TPU v7x, 256 devices: a whole 4x4x8 slice. The times are simulated.
256 devices in a mesh: section: 4 (over y_hi, core), dp: 64 (over x, y_lo, z).
Axes of the slice: x: 4, y: 4 (y_hi: 2, y_lo: 2; y = y_hi * 2 + y_lo), z: 8, core: 2. Of those that a mesh axis runs over, the one named last changes fastest.
Arguments:
- hidden_in: bfloat16 [2, 4096, 3584], P(None, 'dp'), may hold values from -60 to 60
- head_grad: bfloat16 [2, 4096, 3584], P(None, 'dp'), may hold values from -0.4375 to 0.4375
- down_w: bfloat16 [4, 1, 3584, 256], P('section'), may hold values from -0.09375 to 0.09375
- up_w: bfloat16 [4, 1, 3584, 256], P('section'), may hold values from -0.375 to 0.375
- norm_gain: float32 [4, 1, 3584], P('section'), may hold values from 0.1 to 1.9
- codec: bfloat16 [3584, 512], P('dp'), may hold values from -0.0625 to 0.0625
Outputs:
- grad_down: float32 [4, 1, 3584, 256], P('section', None, 'dp')
- grad_up: float32 [4, 1, 3584, 256], P('section', None, 'dp')
- grad_gain: float32 [4, 1, 3584], P('section', None, 'dp')
All inputs are finite; a program needn't handle non-finite values.
Results may differ from a plain program's by a relative error of at most 0.018.
Values may be sent and summed in bfloat16 or wider, within the bound.
A program may use at most 128 MiB of HBM per device.

v0:
```python
import jax
import jax.numpy as jnp
from jax import lax
from jax.sharding import PartitionSpec as P

epsilon = 1e-06


def shifted(value, axis, steps):
    count = lax.axis_size(axis)
    leading, last = (max(0, -steps), min(count, count - steps))
    return lax.ppermute(value, axis, [(source, source + steps) for source in range(leading, last)])


def right_dot(left_side, right_side):
    return lax.dot_general(
        left_side, right_side, (((1,), (1,)), ((), ())), preferred_element_type=jnp.float32
    )


def row_dot(left_side, right_side):
    return lax.dot_general(
        left_side, right_side, (((1,), (1,)), ((0,), (0,))), preferred_element_type=jnp.float32
    )


def on_device(hidden_in, head_grad, down_w, up_w, norm_gain, codec):
    sections = lax.axis_size("section")
    section_index = lax.axis_index("section")
    micro_count, row_count, model_width = hidden_in.shape
    layers = down_w.shape[1]
    latent_width = down_w.shape[3]
    code_width = codec.shape[1]
    code_ratio = model_width / code_width
    down_rows = down_w[0]
    up_rows = up_w[0]
    norm_gains = norm_gain[0]
    codec_full = lax.all_gather(codec, "dp", axis=0, tiled=True)
    is_first = section_index == 0
    is_final = section_index == sections - 1
    span_rows = micro_count * row_count
    tick_count = micro_count + sections - 1

    def keep_rows(stored, fresh_rows, batch_index, is_valid):
        old_rows = lax.dynamic_slice_in_dim(stored, batch_index * row_count, row_count, 1)
        return lax.dynamic_update_slice_in_dim(
            stored, jnp.where(is_valid, fresh_rows, old_rows), batch_index * row_count, 1
        )

    def forward_work(received, batch_index):
        own_rows = lax.dynamic_index_in_dim(hidden_in, batch_index, 0, keepdims=False)
        stream = lax.cond(
            is_first,
            lambda: own_rows.astype(jnp.float32),
            lambda: code_ratio * right_dot(received, codec_full),
        )
        streams, normeds, latents, actives = ([], [], [], [])
        inverse_rms = lax.rsqrt(jnp.mean(stream * stream, axis=-1, keepdims=True) + epsilon)
        normed = (stream * inverse_rms * norm_gains[0]).astype(jnp.bfloat16)
        latent = jnp.dot(normed, down_rows[0], preferred_element_type=jnp.float32)
        active = jax.nn.silu(latent).astype(jnp.bfloat16)
        streams.append(stream)
        normeds.append(normed)
        latents.append(latent)
        actives.append(active)
        stream = stream + right_dot(active, up_rows[0])
        section_out = stream.astype(jnp.bfloat16)
        code_rows = lax.cond(
            is_final,
            lambda: jnp.zeros((row_count, code_width), jnp.bfloat16),
            lambda: jnp.dot(section_out, codec_full, preferred_element_type=jnp.float32).astype(
                jnp.bfloat16
            ),
        )
        return (
            jnp.stack(streams),
            jnp.stack(normeds),
            jnp.stack(latents),
            jnp.stack(actives),
            code_rows,
        )

    def forward_skip(received, batch_index):
        return (
            jnp.zeros((layers, row_count, model_width), jnp.float32),
            jnp.zeros((layers, row_count, model_width), jnp.bfloat16),
            jnp.zeros((layers, row_count, latent_width), jnp.float32),
            jnp.zeros((layers, row_count, latent_width), jnp.bfloat16),
            jnp.zeros((row_count, code_width), jnp.bfloat16),
        )

    kept_state = jnp.zeros((layers, span_rows, model_width), jnp.float32)
    kept_normed = jnp.zeros((layers, span_rows, model_width), jnp.bfloat16)
    kept_latent = jnp.zeros((layers, span_rows, latent_width), jnp.float32)
    kept_active = jnp.zeros((layers, span_rows, latent_width), jnp.bfloat16)
    received = jnp.zeros((row_count, code_width), jnp.bfloat16)
    for tick_step in range(tick_count):
        slot_index = tick_step - section_index
        is_valid = jnp.logical_and(slot_index >= 0, slot_index < micro_count)
        batch_index = jnp.clip(slot_index, 0, micro_count - 1)
        results = lax.cond(is_valid, forward_work, forward_skip, received, batch_index)
        kept_state = keep_rows(kept_state, results[0], batch_index, is_valid)
        kept_normed = keep_rows(kept_normed, results[1], batch_index, is_valid)
        kept_latent = keep_rows(kept_latent, results[2], batch_index, is_valid)
        kept_active = keep_rows(kept_active, results[3], batch_index, is_valid)
        if tick_step + 1 < tick_count:
            received = shifted(results[4], "section", 1)

    def backward_work(received, batch_index):
        own_rows = lax.dynamic_index_in_dim(head_grad, batch_index, 0, keepdims=False)
        gradient = lax.cond(
            is_final, lambda: own_rows.astype(jnp.float32), lambda: right_dot(received, codec_full)
        )
        start_row = batch_index * row_count
        streams = lax.dynamic_slice_in_dim(kept_state, start_row, row_count, 1)
        latents = lax.dynamic_slice_in_dim(kept_latent, start_row, row_count, 1)
        grad_list = [None] * layers
        dlat_list = [None] * layers
        gain_list = [None] * layers
        for layer_index in reversed(range(layers)):
            stream = streams[layer_index]
            latent = latents[layer_index]
            inverse_rms = lax.rsqrt(jnp.mean(stream * stream, axis=-1, keepdims=True) + epsilon)
            grad_rows = gradient.astype(jnp.bfloat16)
            d_active = jnp.dot(grad_rows, up_rows[layer_index], preferred_element_type=jnp.float32)
            sigmoid_value = jax.nn.sigmoid(latent)
            d_latent = (d_active * sigmoid_value * (1.0 + latent * (1.0 - sigmoid_value))).astype(
                jnp.bfloat16
            )
            d_normed = right_dot(d_latent, down_rows[layer_index])
            weighted = d_normed * norm_gains[layer_index]
            cube = inverse_rms * inverse_rms * inverse_rms
            gradient = (
                gradient
                + inverse_rms * weighted
                - stream * cube * jnp.mean(weighted * stream, axis=-1, keepdims=True)
            )
            grad_list[layer_index] = grad_rows
            dlat_list[layer_index] = d_latent
            gain_list[layer_index] = jnp.sum(d_normed * stream * inverse_rms, axis=0)
        grad_entry = gradient.astype(jnp.bfloat16)
        back_code = lax.cond(
            is_first,
            lambda: jnp.zeros((row_count, code_width), jnp.bfloat16),
            lambda: (
                code_ratio * jnp.dot(grad_entry, codec_full, preferred_element_type=jnp.float32)
            ).astype(jnp.bfloat16),
        )
        return (jnp.stack(grad_list), jnp.stack(dlat_list), jnp.stack(gain_list), back_code)

    def backward_skip(received, batch_index):
        return (
            jnp.zeros((layers, row_count, model_width), jnp.bfloat16),
            jnp.zeros((layers, row_count, latent_width), jnp.bfloat16),
            jnp.zeros((layers, model_width), jnp.float32),
            jnp.zeros((row_count, code_width), jnp.bfloat16),
        )

    kept_gradb = jnp.zeros((layers, span_rows, model_width), jnp.bfloat16)
    kept_dlatent = jnp.zeros((layers, span_rows, latent_width), jnp.bfloat16)
    gain_total = jnp.zeros((layers, model_width), jnp.float32)
    received = jnp.zeros((row_count, code_width), jnp.bfloat16)
    for tick_step in range(tick_count):
        slot_index = tick_step - (sections - 1 - section_index)
        is_valid = jnp.logical_and(slot_index >= 0, slot_index < micro_count)
        batch_index = jnp.clip(slot_index, 0, micro_count - 1)
        results = lax.cond(is_valid, backward_work, backward_skip, received, batch_index)
        kept_gradb = keep_rows(kept_gradb, results[0], batch_index, is_valid)
        kept_dlatent = keep_rows(kept_dlatent, results[1], batch_index, is_valid)
        gain_total = gain_total + jnp.where(is_valid, results[2], jnp.zeros_like(results[2]))
        if tick_step + 1 < tick_count:
            received = shifted(results[3], "section", -1)
    local_down = row_dot(kept_normed, kept_dlatent)
    local_up = row_dot(kept_gradb, kept_active)
    sum_down, sum_up, sum_gain = (
        lax.psum_scatter(local_down, "dp", scatter_dimension=1, tiled=True),
        lax.psum_scatter(local_up, "dp", scatter_dimension=1, tiled=True),
        lax.psum_scatter(gain_total, "dp", scatter_dimension=1, tiled=True),
    )
    return (sum_down[None], sum_up[None], sum_gain[None])


def solution(mesh):
    in_specs = (
        P(None, "dp", None),
        P(None, "dp", None),
        P("section", None, None, None),
        P("section", None, None, None),
        P("section", None, None),
        P("dp", None),
    )
    out_specs = (
        P("section", None, "dp", None),
        P("section", None, "dp", None),
        P("section", None, "dp"),
    )
    return jax.shard_map(
        on_device, mesh=mesh, in_specs=in_specs, out_specs=out_specs, check_vma=False
    )
```

profile of v0, /device:TPU:16, one launch (start us, length us, event | category | flops | bytes accessed | tf_op | source)
XLA Modules:
  0.0 1140.8 jit_solution(12805809360414853790)
XLA Ops:
  8.0 307.3 %all-gather.2.cloned.1.call-done = bf16[3584,512]{1,0:T(8,128)(2,1)} async-done(((bf16[56,512]{1,0:T(8,128)(2,1)}), bf16[3584,512]{1,0:T(8,128)(2,1)}) %all-gather.2.cloned.1.call-update) | async-done | bytes 3670032 | tf_op jit(solution)/shard_map/all_gather | solution.py:38
  320.0 5.0 collective-permute-done
  325.0 3.1 conditional.29
  332.2 20.5 %collective-permute-done.1 = bf16[64,512]{1,0:T(8,128)(2,1)S(1)} collective-permute-done((bf16[64,512]{1,0:T(8,128)(2,1)}, bf16[64,512]{1,0:T(8,128)(2,1)S(1)}, u32[]{:S(2)}, u32[]{:S(2)}) %collective-permute-start.1) | collective-permute-done | bytes 65568 | tf_op jit(solution)/shard_map/ppermute | solution.py:12
  352.8 15.7 %conditional.30 = (f32[1,64,3584]{2,1,0:T(8,128)}, bf16[1,64,3584]{2,1,0:T(8,128)(2,1)}, f32[1,64,256]{2,1,0:T(8,128)}, bf16[1,64,256]{2,1,0:T(8,128)(2,1)S(1)}, bf16[64,512]{1,0:T(8,128)(2,1)}) conditional(s32[]{:T(128)} %convert_element_type.289, () %tuple.275, (pred[]{:T(512)}, bf16[64,512]{1,0:T(8,128)(2,1)S(1)}, bf16[3584,512]{1,0:T(8,128)(2,1)}, ...), branch_computations={%region_16.17_spmd, %region_17.0_spmd} | conditional | flops 707362880 | bytes 32990682 | solution.py:101
  352.8 4.3 conditional.4
  352.8 3.4 multiply_reduce_fusion.4
  362.0 3.4 conditional.5
  362.0 3.4 convolution_convert_fusion.2
  375.7 15.7 %conditional.31 = (f32[1,64,3584]{2,1,0:T(8,128)}, bf16[1,64,3584]{2,1,0:T(8,128)(2,1)}, f32[1,64,256]{2,1,0:T(8,128)}, bf16[1,64,256]{2,1,0:T(8,128)(2,1)S(1)}, bf16[64,512]{1,0:T(8,128)(2,1)}) conditional(s32[]{:T(128)} %convert_element_type.290, () %tuple.277, (pred[]{:T(512)}, bf16[64,512]{1,0:T(8,128)(2,1)S(1)}, bf16[3584,512]{1,0:T(8,128)(2,1)}, ...), branch_computations={%region_24.25_spmd, %region_25.0_spmd} | conditional | flops 707362880 | bytes 32990682 | solution.py:101
  375.7 4.3 conditional.6
  375.7 3.4 multiply_reduce_fusion.6
  385.0 3.4 conditional.7
  385.0 3.4 convolution_convert_fusion.3
  393.3 2.5 select_dynamic-update-slice_fusion.1
  406.6 17.1 %collective-permute-done.4 = bf16[64,512]{1,0:T(8,128)(2,1)S(1)} collective-permute-done((bf16[64,512]{1,0:T(8,128)(2,1)}, bf16[64,512]{1,0:T(8,128)(2,1)S(1)}, u32[]{:S(2)}, u32[]{:S(2)}) %collective-permute-start.4) | collective-permute-done | bytes 65568 | tf_op jit(solution)/shard_map/ppermute | solution.py:12
  423.8 13.5 %conditional.34 = (bf16[1,64,3584]{2,1,0:T(8,128)(2,1)}, bf16[1,64,256]{2,1,0:T(8,128)(2,1)S(1)}, f32[1,3584]{1,0:T(1,128)S(1)}, bf16[64,512]{1,0:T(8,128)(2,1)}) conditional(s32[]{:T(128)} %convert_element_type.293, () %tuple.283, (pred[]{:T(512)}, bf16[64,512]{1,0:T(8,128)(2,1)S(1)}, bf16[3584,512]{1,0:T(8,128)(2,1)}, s32[]{:T(128)}, ...), branch_computations={%region_47.48_spmd, %region_48.0_spmd} | conditional | flops 708752064 | bytes 38704184 | solution.py:167
  423.8 4.2 conditional.11
  423.8 4.2 fusion.163
  433.8 3.4 conditional.12
  433.8 3.4 fusion.6
  441.4 15.3 %conditional.35 = (bf16[1,64,3584]{2,1,0:T(8,128)(2,1)}, bf16[1,64,256]{2,1,0:T(8,128)(2,1)S(1)}, f32[1,3584]{1,0:T(1,128)}, bf16[64,512]{1,0:T(8,128)(2,1)}) conditional(s32[]{:T(128)} %convert_element_type.294, () %tuple.285, (pred[]{:T(512)}, bf16[64,512]{1,0:T(8,128)(2,1)S(1)}, bf16[3584,512]{1,0:T(8,128)(2,1)}, s32[]{:T(128)}, ...), branch_computations={%region_56.57_spmd, %region_57.0_spmd} | conditional | flops 708752064 | bytes 38706288 | solution.py:167
  441.4 4.2 conditional.13
  441.4 4.2 fusion.164
  452.7 3.4 conditional.14
  452.7 3.4 fusion.7
  456.7 5.1 collective-permute-start.6
  466.1 18.4 %collective-permute-start.7 = (bf16[64,512]{1,0:T(8,128)(2,1)}, bf16[64,512]{1,0:T(8,128)(2,1)S(1)}, u32[]{:S(2)}, u32[]{:S(2)}) collective-permute-start(bf16[64,512]{1,0:T(8,128)(2,1)} %get-tuple-element.831), channel_id=1, source_target_pairs={{64,0},{128,64},{192,128},{65,1},{129,65},{193,129},{66,2},{130,66... | collective-permute-start | bytes 196616 | tf_op jit(solution)/shard_map/ppermute | solution.py:12
  489.3 3.6 convolution_bitcast_fusion
  502.1 308.4 %all-reduce = f32[1,3584]{1,0:T(1,128)S(1)} all-reduce(f32[1,3584]{1,0:T(1,128)S(1)} %fusion.162), channel_id=4, replica_groups=mesh['section'=4,'dp'=64] {'dp'}, use_global_device_ids=true, to_apply=%region_82.83.clone | all-reduce | flops 3584 | bytes 28672
  811.1 4.9 reduce-scatter.6.cloned.1.call-done
  816.0 318.3 %reduce-scatter.4.cloned.1.call-done = f32[1,56,256]{2,1,0:T(8,128)} async-done(((f32[1,3584,256]{2,1,0:T(8,128)}), f32[1,56,256]{2,1,0:T(8,128)}) %reduce-scatter.4.cloned.1.call-update) | async-done | bytes 57360 | tf_op jit(solution)/shard_map/reduce_scatter | solution.py:176
  (188 shorter events, 93.7 us)
Async XLA Ops:
  7.2 308.2 %all-gather.2.cloned.1.call-start = ((), (), s32[]{:S(2)}) async-start(), calls=%async_computation.2 | async-start | bytes 3727360 | tf_op jit(solution)/shard_map/all_gather | solution.py:38
  7.9 808.1 %reduce-scatter.6.cloned.1.call-start = ((), (), s32[]{:S(2)}) async-start(), calls=%async_computation.4 | async-start | bytes 3727360 | tf_op jit(solution)/shard_map/reduce_scatter | solution.py:177
  317.7 2.2 copy-start.27
  317.7 7.3 collective-permute-start
  319.6 5.4 copy-start
  319.6 5.4 copy-start.16
  319.6 5.4 copy-start.33
  319.9 5.1 copy-start.2
  328.1 24.7 %collective-permute-start.1 = (bf16[64,512]{1,0:T(8,128)(2,1)}, bf16[64,512]{1,0:T(8,128)(2,1)S(1)}, u32[]{:S(2)}, u32[]{:S(2)}) collective-permute-start(bf16[64,512]{1,0:T(8,128)(2,1)} %get-tuple-element.808), channel_id=1, source_target_pairs={{0,64},{64,128},{128,192},{1,65},{65,129},{129,193},{2,66},{66,130... | collective-permute-start | bytes 196616 | tf_op jit(solution)/shard_map/ppermute | solution.py:12
  358.1 2.5 copy-start.14
  358.1 2.5 copy-start.21
  368.5 7.3 collective-permute-start.2
  381.0 2.5 copy-start.15
  381.0 2.5 copy-start.23
  391.4 7.3 collective-permute-start.3
  400.4 2.5 copy-start.44
  400.4 2.5 copy-start.29
  404.1 2.3 copy-start.32
  404.1 2.4 copy-start.45
  404.1 19.6 %collective-permute-start.4 = (bf16[64,512]{1,0:T(8,128)(2,1)}, bf16[64,512]{1,0:T(8,128)(2,1)S(1)}, u32[]{:S(2)}, u32[]{:S(2)}) collective-permute-start(bf16[64,512]{1,0:T(8,128)(2,1)} %get-tuple-element.825), channel_id=1, source_target_pairs={{64,0},{128,64},{192,128},{65,1},{129,65},{193,129},{66,2},{130,66... | collective-permute-start | bytes 196616 | tf_op jit(solution)/shard_map/ppermute | solution.py:12
  427.9 2.4 copy-start.5
  430.3 2.4 copy-start.35
  433.8 3.4 copy-start.36
  437.3 4.1 copy-start.46
  437.3 4.1 collective-permute-start.5
  445.6 2.4 copy-start.7
  447.9 2.9 copy-start.37
  448.7 2.2 copy-start.51
  452.7 4.0 copy-start.38
  456.7 7.3 collective-permute-start.6
  466.1 20.6 %collective-permute-start.7 = (bf16[64,512]{1,0:T(8,128)(2,1)}, bf16[64,512]{1,0:T(8,128)(2,1)S(1)}, u32[]{:S(2)}, u32[]{:S(2)}) collective-permute-start(bf16[64,512]{1,0:T(8,128)(2,1)} %get-tuple-element.831), channel_id=1, source_target_pairs={{64,0},{128,64},{192,128},{65,1},{129,65},{193,129},{66,2},{130,66... | collective-permute-start | bytes 196616 | tf_op jit(solution)/shard_map/ppermute | solution.py:12
  493.0 641.4 %reduce-scatter.4.cloned.1.call-start = ((), (), s32[]{:S(2)}) async-start(), calls=%async_computation.3 | async-start | bytes 3727360 | tf_op jit(solution)/shard_map/reduce_scatter | solution.py:176
  (13 other events, 20.3 us)
Sparse Core Ops, SparseCore 0:
  9.8 305.5 all-gather.1
  493.1 322.9 reduce-scatter.5
  819.3 314.9 reduce-scatter.3
where the time goes:
time: 1140 us
  waiting for transfers between devices  681 us (60%)
  blocking collectives  308 us (27%)
  matrix products  51.7 us (5%)
  starting transfers between devices  35.4 us (3%)
  other arithmetic  28.6 us (3%)
  local copies, waits for them, and re-layouts  20.3 us (2%)
  between operations  14.9 us (1%)
    reduce_scatter x1, waiting for transfers between devices, on_device(): lax.psum_scatter(local_down, 'dp', scatter_dimension=1, tiled=True)  318 us
    unnamed x1, blocking collectives  308 us
    all_gather x1, waiting for transfers between devices, on_device(): codec_full = lax.all_gather(codec, 'dp', axis=0, tiled=True)  307 us
    ppermute x8, waiting for transfers between devices, shifted(): lax.ppermute(value, axis, [(source, source + steps) for source in range(l...  49.7 us
    ppermute x8, starting transfers between devices, shifted(): lax.ppermute(value, axis, [(source, source + steps) for source in range(l...  35.3 us
  transfers between devices with their start and end apart: 11, of which 11 were waited for; matrix products, arithmetic and copies ran while one was open for 2% of the time, Pallas kernels for 0%

commit v1 on v0

v1 whole, which is shorter than its diff:
```python
import functools

import jax
import jax.numpy as jnp
from jax import lax
from jax.experimental import pallas as pl
from jax.experimental.pallas import tpu as pltpu
from jax.sharding import PartitionSpec as P

epsilon = 1e-06
y_size, z_size = 2, 8
f32, bf16 = jnp.float32, jnp.bfloat16
mesh_ids = pl.DeviceIdType.MESH


def plain_dot(left, right):
    return lax.dot_general(left, right, (((1,), (0,)), ((), ())), preferred_element_type=f32)


def right_dot(left, right):
    return lax.dot_general(left, right, (((1,), (1,)), ((), ())), preferred_element_type=f32)


def left_dot(left, right):
    return lax.dot_general(left, right, (((0,), (0,)), ((), ())), preferred_element_type=f32)


def sigmoid(value):
    return 1.0 / (1.0 + jnp.exp(-value))


def silu_slope(latent):
    gate = sigmoid(latent)
    return gate * (1.0 + latent * (1.0 - gate))


def kernel(
    sizes,
    hidden,
    head,
    down_hbm,
    up_hbm,
    gain,
    codec,
    out_down,
    out_up,
    out_gain,
    tok,
    down,
    up,
    down32,
    gain_col,
    gdown,
    planes,
    flat,
    acc,
    weights,
    tok_code,
    latent_ref,
    active_ref,
    inv_ref,
    slope_ref,
    code_grid,
    code_in,
    code_out,
    back_in,
    back_out,
    wide_in,
    factor,
    factor_in,
    big,
    y_send,
    y_in,
    z_send,
    z_in,
    part,
    sum_a_send,
    sum_a_in,
    sum_z_send,
    sum_z_in,
    sum_g,
    local_sem,
    send_sem,
    recv_sem,
):
    X, Y, Z = sizes
    micro, rows, D = hidden.shape
    R = micro * rows
    C, K = codec.shape[1], down.shape[1]
    own = codec.shape[0]
    lanes = C // 4
    chunk = D // X
    ratio = D / C
    sec = lax.axis_index("section")
    dp = lax.axis_index("dp")
    core = lax.rem(sec, 2)
    x = dp // (Y * Z)
    y = lax.rem(dp // Z, Y)
    z = lax.rem(dp, Z)
    xy = dp // Z
    other_y = 1 - y
    far_sec = lax.rem(sec + 2, 4)
    sibling = sec + 1 - 2 * core
    ends = jnp.logical_or(sec == 0, sec == 3)
    middle = jnp.logical_not(ends)

    def place(px, py, pz):
        return (px * Y + py) * Z + pz

    def ring(mine, count):
        return [lax.rem(mine + off, count) for off in range(1, count)]

    names = [
        ("x0", X), ("z0", Z), ("y0", 2), ("z1", Z), ("y1", 2), ("x1", X), ("d0", 2), ("d1", X),
        ("code", 1), ("back", 1), ("wide", X), ("factor", X), ("big_y", 1), ("big_z", Z),
        ("sum_a", X * Y), ("sum_z", Z), ("sum_g", X * Y),
    ]
    base, total = {}, 0
    for name, count in names:
        base[name] = total
        total += count
    sent = [0]

    def start(src, dst, name, index, section, place_at, slot=None):
        if slot is None:
            slot = sent[0]
            sent[0] += 1
        copy = pltpu.make_async_remote_copy(
            src_ref=src, dst_ref=dst, send_sem=send_sem.at[slot],
            recv_sem=recv_sem.at[base[name] + index],
            device_id=(section, place_at), device_id_type=mesh_ids,
        )
        copy.start()
        return copy

    def left(src, slot):
        pltpu.make_async_remote_copy(
            src_ref=src, dst_ref=src, send_sem=send_sem.at[slot], recv_sem=recv_sem.at[0],
            device_id=(sec, dp), device_id_type=mesh_ids,
        ).wait_send()

    def arrive(dst, name, index):
        pltpu.make_async_remote_copy(
            src_ref=dst, dst_ref=dst, send_sem=send_sem.at[0],
            recv_sem=recv_sem.at[base[name] + index],
            device_id=(sec, dp), device_id_type=mesh_ids,
        ).wait_recv()

    load_down = pltpu.make_async_copy(down_hbm, down, local_sem.at[0])
    load_up = pltpu.make_async_copy(up_hbm, up, local_sem.at[1])
    load_hidden = pltpu.make_async_copy(hidden, tok, local_sem.at[2])
    load_head = pltpu.make_async_copy(head, tok, local_sem.at[2])
    load_down.start()
    load_up.start()
    pl.when(sec == 0)(load_hidden.start)
    pl.when(sec == 3)(load_head.start)

    color0, color1 = 2 * core, 2 * core + 1

    @pl.when(core == 0)
    def _():
        planes[0, x, y, z] = codec[:, 0:lanes]
        planes[1, x, y, z] = codec[:, lanes : 2 * lanes]

    @pl.when(core == 1)
    def _():
        planes[2, x, y, z] = codec[:, 2 * lanes : 3 * lanes]
        planes[3, x, y, z] = codec[:, 3 * lanes :]

    barrier = pltpu.get_barrier_semaphore()
    peers = [(sec, place(x, y, pz)) for pz in ring(z, Z)]
    xy_ring = ring(xy, X * Y)
    peers += [(sec, pxy * Z + z) for pxy in xy_ring]
    peers += [(sibling, dp), (far_sec, place(x, other_y, z)), (3 - sec, dp)]
    for peer in peers:
        pl.semaphore_signal(barrier, inc=1, device_id=peer, device_id_type=mesh_ids)
    pl.semaphore_wait(barrier, len(peers))

    half_x, half_z = X // 2, Z // 2
    copies = []
    mine = planes.at[color0, x, y, z]
    for px in ring(x, X):
        copies.append(start(mine, mine, "x0", x, sec, place(px, y, z)))
    mine = planes.at[color1, x, y, z]
    for pz in ring(z, Z):
        copies.append(start(mine, mine, "z1", z, sec, place(x, y, pz)))

    load_down.wait()
    step = 128

    def scale_rows(index, carry):
        at = pl.ds(pl.multiple_of(index * step, step), step)
        column = jnp.broadcast_to(gain[:, at], (step, step)).T
        gain_col[at, :] = column
        wide = down[at, :].astype(f32)
        down32[at, :] = wide
        parts = [wide[:, k : k + step] * column[:, : min(step, K)] for k in range(0, K, step)]
        gdown[at, :] = jnp.concatenate(parts, axis=1).astype(bf16)
        return carry

    for px in ring(x, X):
        arrive(planes.at[color0, px, y, z], "x0", px)
    line = planes.at[color0, :, y, z]
    for pz in ring(z, Z):
        copies.append(start(line, line, "z0", z, sec, place(x, y, pz)))

    lax.fori_loop(0, D // step, scale_rows, 0)

    for pz in ring(z, Z):
        arrive(planes.at[color1, x, y, pz], "z1", pz)
    near, far = planes.at[color1, x, y, 0:half_z], planes.at[color1, x, y, half_z:Z]
    copies.append(start(near, near, "y1", 0, sec, place(x, other_y, z)))
    copies.append(start(far, far, "y1", 1, far_sec, place(x, other_y, z)))

    load_up.wait()

    @pl.when(sec == 0)
    def _():
        load_hidden.wait()

        def squares(index, carry):
            at = pl.ds(pl.multiple_of(index * chunk, chunk), chunk)
            value = tok[:, :, at].reshape(R, chunk).astype(f32)
            return carry + jnp.sum(value * value, axis=-1, keepdims=True)

        square = lax.fori_loop(0, X, squares, jnp.zeros((R, 1), f32))
        inverse = lax.rsqrt(square / D + epsilon)
        inv_ref[...] = inverse

        def project(index, carry):
            at = pl.ds(pl.multiple_of(index * chunk, chunk), chunk)
            value = tok[:, :, at].reshape(R, chunk).astype(f32)
            normed = (value * inverse * gain[:, at]).astype(bf16)
            return carry + plain_dot(normed, down[at, :])

        latent = lax.fori_loop(0, X, project, jnp.zeros((R, K), f32))
        active_ref[...] = (latent * sigmoid(latent)).astype(bf16)
        slope_ref[...] = silu_slope(latent)

    @pl.when(sec == 3)
    def _():
        load_head.wait()

        def project(index, carry):
            at = pl.ds(pl.multiple_of(index * chunk, chunk), chunk)
            return carry + plain_dot(tok[:, :, at].reshape(R, chunk), up[at, :])

        latent_ref[...] = lax.fori_loop(0, X, project, jnp.zeros((R, K), f32))

    for pz in ring(z, Z):
        arrive(planes.at[color0, :, y, pz], "z0", pz)
    near, far = planes.at[color0, 0:half_x, y], planes.at[color0, half_x:X, y]
    copies.append(start(near, near, "y0", 0, sec, place(x, other_y, z)))
    copies.append(start(far, far, "y0", 1, far_sec, place(x, other_y, z)))
    half = planes.at[color0, :, y]
    copies.append(start(half, half, "d0", 0, sibling, dp))

    arrive(planes.at[color1, x, other_y, 0:half_z], "y1", 0)
    arrive(planes.at[color1, x, other_y, half_z:Z], "y1", 1)
    slab = planes.at[color1, x]
    for px in ring(x, X):
        copies.append(start(slab, slab, "x1", x, sec, place(px, y, z)))
    copies.append(start(slab, slab, "d1", x, sibling, dp))

    arrive(planes.at[color0, 0:half_x, other_y], "y0", 0)
    arrive(planes.at[color0, half_x:X, other_y], "y0", 1)
    half = planes.at[color0, :, other_y]
    copies.append(start(half, half, "d0", 1, sibling, dp))
    for px in ring(x, X):
        slab = planes.at[color1, px]
        arrive(slab, "x1", px)
        copies.append(start(slab, slab, "d1", px, sibling, dp))

    their0, their1 = 2 - 2 * core, 3 - 2 * core
    arrive(planes.at[their0, :, y], "d0", 0)
    arrive(planes.at[their0, :, other_y], "d0", 1)
    arrive(planes.at[their1, x], "d1", x)
    for px in ring(x, X):
        arrive(planes.at[their1, px], "d1", px)

    wide_slot = sent[0]
    sent[0] += X - 1

    @pl.when(ends)
    def _():
        for off, px in enumerate(ring(x, X)):
            at = pl.ds(pl.multiple_of(px * chunk, chunk), chunk)
            start(
                tok.at[:, :, at], wide_in.at[x], "wide", x, sec, place(px, y, z), wide_slot + off
            )

    acc[...] = jnp.zeros_like(acc)

    @pl.when(ends)
    def _():
        tok_code[...] = jnp.zeros_like(tok_code)

    def products(index, carry):
        at = pl.ds(pl.multiple_of(index * chunk, chunk), chunk)
        for color in range(4):
            piece = planes[color, index].astype(f32).reshape(chunk, lanes).astype(bf16)
            flat[:, color * lanes : (color + 1) * lanes] = piece
        block = flat[...]

        @pl.when(sec != 3)
        def _():
            acc[:, K + C :] += left_dot(block, up[at, :])

        @pl.when(sec != 0)
        def _():
            acc[:, 0:K] += left_dot(block, gdown[at, :])
            acc[:, K : K + C] += left_dot(block, block)

        @pl.when(ends)
        def _():
            tok_code[...] += plain_dot(tok[:, :, at].reshape(R, chunk), block)

        return carry

    lax.fori_loop(0, X, products, 0)
    weights[...] = acc[...].astype(bf16)

    def forward():
        code = code_in[...]
        both = plain_dot(code, weights[:, 0 : K + C])
        grid = both[:, K:]
        square = jnp.sum(code.astype(f32) * grid, axis=-1, keepdims=True) * (ratio * ratio / D)
        inverse = lax.rsqrt(square + epsilon)
        latent = ratio * inverse * both[:, 0:K]
        active = (latent * sigmoid(latent)).astype(bf16)
        return code, grid, inverse, latent, active

    def backward(inner, grid, inverse, latent, d_latent):
        weight = jnp.sum(d_latent.astype(f32) * latent, axis=-1, keepdims=True)
        weight = weight * inverse * inverse * (ratio / D)
        through = right_dot(d_latent, weights[:, 0:K])
        return (ratio * (inner + inverse * through - weight * grid)).astype(bf16)

    hops = []

    @pl.when(sec == 0)
    def _():
        result = tok_code[...] + right_dot(active_ref[...], weights[:, K + C :])
        code_out[...] = result.astype(bf16)
        start(code_out, code_in, "code", 0, 1, dp).wait_send()

    @pl.when(middle)
    def _():
        arrive(code_in, "code", 0)
        code, grid, inverse, latent, active = forward()
        result = ratio * grid + right_dot(active, weights[:, K + C :])
        code_out[...] = result.astype(bf16)
        hop = start(code_out, code_in, "code", 0, sec + 1, dp)
        code_grid[...] = grid
        inv_ref[...] = inverse
        latent_ref[...] = latent
        active_ref[...] = active
        slope_ref[...] = silu_slope(latent)
        hop.wait_send()

    def send_factor():
        result = []
        for px in ring(x, X):
            result.append(start(factor, factor_in.at[x], "factor", x, sec, place(px, y, z)))
        return result

    @pl.when(sec == 3)
    def _():
        arrive(code_in, "code", 0)
        code, grid, inverse, latent, active = forward()
        factor[...] = active
        d_latent = (latent_ref[...] * silu_slope(latent)).astype(bf16)
        back_out[...] = backward(tok_code[...], grid, inverse, latent, d_latent)
        hop = start(back_out, back_in, "back", 0, 2, dp)
        scaled = (d_latent.astype(f32) * (ratio * inverse)).astype(bf16)
        part[:, 0:K] = left_dot(code, scaled)
        hop.wait_send()

    @pl.when(middle)
    def _():
        arrive(back_in, "back", 0)
        back = back_in[...]
        both = plain_dot(back, weights[:, K:])
        inverse = inv_ref[...]
        d_latent = (both[:, C:] * slope_ref[...]).astype(bf16)
        back_out[...] = backward(both[:, 0:C], code_grid[...], inverse, latent_ref[...], d_latent)
        hop = start(back_out, back_in, "back", 0, sec - 1, dp)
        scaled = (d_latent.astype(f32) * (ratio * inverse)).astype(bf16)
        part[:, 0:K] = left_dot(code_in[...], scaled)
        part[:, K:] = left_dot(back, active_ref[...])
        hop.wait_send()

    @pl.when(sec == 0)
    def _():
        arrive(back_in, "back", 0)
        back = back_in[...]
        d_latent = (plain_dot(back, weights[:, K + C :]) * slope_ref[...]).astype(bf16)
        factor[...] = (d_latent.astype(f32) * inv_ref[...]).astype(bf16)
        part[:, 0:K] = left_dot(back, active_ref[...])

    block_rows = C // (X * Y)

    def sum_scatter(width):
        sum_a_send[:, :, 0:width] = part[:, 0:width].astype(bf16).reshape(X * Y, block_rows, width)
        result = []
        for pxy in xy_ring:
            result.append(
                start(sum_a_send.at[pxy, :, 0:width], sum_a_in.at[xy, :, 0:width], "sum_a", xy, sec, pxy * Z + z)
            )
        return result

    def sum_line(width):
        value = sum_a_send[xy, :, 0:width].astype(f32)
        for pxy in xy_ring:
            arrive(sum_a_in.at[pxy, :, 0:width], "sum_a", pxy)
            value = value + sum_a_in[pxy, :, 0:width].astype(f32)
        sum_z_send[:, 0:width] = value.astype(bf16)
        result = []
        for pz in ring(z, Z):
            result.append(
                start(sum_z_send.at[:, 0:width], sum_z_in.at[z, :, 0:width], "sum_z", z, sec, place(x, y, pz))
            )
        return result, value

    def sum_gather(width, value):
        for pz in ring(z, Z):
            arrive(sum_z_in.at[pz, :, 0:width], "sum_z", pz)
            value = value + sum_z_in[pz, :, 0:width].astype(f32)
        sum_g[xy, :, 0:width] = value.astype(bf16)
        result = []
        mine = sum_g.at[xy, :, 0:width]
        for pxy in xy_ring:
            result.append(start(mine, mine, "sum_g", xy, sec, pxy * Z + z))
        return result

    def sum_end(width):
        for pxy in xy_ring:
            arrive(sum_g.at[pxy, :, 0:width], "sum_g", pxy)
        return sum_g[:, :, 0:width].reshape(C, width)

    own_rows = pl.ds(pl.multiple_of(dp * own, 8), own)

    def put_down(value):
        column = gain_col[own_rows, :]
        weighted = down32[own_rows, :] * value
        folded = weighted[:, 0 : min(step, K)]
        for k in range(step, K, step):
            folded = folded + weighted[:, k : k + step]
        if own < step:
            folded = jnp.concatenate([folded, jnp.zeros((step - own, folded.shape[1]), f32)], axis=0)
        out_gain[...] = jnp.sum(folded.T, axis=0, keepdims=True)[:, 0:own]
        for k in range(0, K, step):
            out_down[:, k : k + step] = value[:, k : k + step] * column[:, : min(step, K)]

    @pl.when(middle)
    def _():
        waits = sum_scatter(2 * K)
        more, value = sum_line(2 * K)
        waits += more
        waits += sum_gather(2 * K, value)
        result = plain_dot(codec[...], sum_end(2 * K))
        put_down(result[:, 0:K])
        out_up[...] = result[:, K:]
        for copy in waits:
            copy.wait_send()

    @pl.when(ends)
    def _():
        waits = send_factor()
        waits += sum_scatter(K)
        at = pl.ds(pl.multiple_of(x * chunk, chunk), chunk)
        big[...] = left_dot(tok[:, :, at].reshape(R, chunk), factor[...])
        for px in ring(x, X):
            arrive(wide_in.at[px], "wide", px)
            arrive(factor_in.at[px], "factor", px)
            big[...] += left_dot(wide_in[px].reshape(R, chunk), factor_in[px])
        y_rows = chunk // Y
        their_rows = pl.ds(pl.multiple_of(other_y * y_rows, 8), y_rows)
        my_rows = pl.ds(pl.multiple_of(y * y_rows, 8), y_rows)
        y_send[...] = big[their_rows, :].astype(bf16)
        waits.append(start(y_send, y_in, "big_y", 0, sec, place(x, other_y, z)))
        more, value = sum_line(K)
        waits += more
        arrive(y_in, "big_y", 0)
        line_sum = (big[my_rows, :] + y_in[...].astype(f32)).reshape(Z, own, K)
        z_send[...] = line_sum.astype(bf16)
        for pz in ring(z, Z):
            waits.append(start(z_send.at[pz], z_in.at[z], "big_z", z, sec, place(x, y, pz)))
        waits += sum_gather(K, value)
        wide_sum = z_send[z].astype(f32)
        for pz in ring(z, Z):
            arrive(z_in.at[pz], "big_z", pz)
            wide_sum = wide_sum + z_in[pz].astype(f32)
        result = plain_dot(codec[...], sum_end(K))

        @pl.when(sec == 0)
        def _():
            put_down(wide_sum)
            out_up[...] = result

        @pl.when(sec == 3)
        def _():
            put_down(result)
            out_up[...] = wide_sum

        for copy in waits:
            copy.wait_send()
        for off in range(X - 1):
            left(wide_in.at[x], wide_slot + off)

    for copy in copies:
        copy.wait_send()


def on_device(hidden_in, head_grad, down_w, up_w, norm_gain, codec):
    micro, rows, D = hidden_in.shape
    K, C, own = down_w.shape[3], codec.shape[1], codec.shape[0]
    Y, Z = y_size, z_size
    X = lax.axis_size("dp") // (Y * Z)
    R, chunk, lanes = micro * rows, D // X, C // 4
    block_rows = C // (X * Y)
    any_space = pl.BlockSpec(memory_space=pl.ANY)
    vmem = pl.BlockSpec(memory_space=pltpu.VMEM)
    recv_count = 4 * X + 4 * Z + 10 + 2 * X * Y + 8
    scratch = [
        ((micro, rows, D), bf16),
        ((D, K), bf16),
        ((D, K), bf16),
        ((D, K), f32),
        ((D, 128), f32),
        ((D, K), bf16),
        ((4, X, Y, Z, own, lanes), bf16),
        ((chunk, C), bf16),
        ((C, 2 * K + C), f32),
        ((C, 2 * K + C), bf16),
        ((R, C), f32),
        ((R, K), f32),
        ((R, K), bf16),
        ((R, 1), f32),
        ((R, K), f32),
        ((R, C), f32),
        ((R, C), bf16),
        ((R, C), bf16),
        ((R, C), bf16),
        ((R, C), bf16),
        ((X, micro, rows, chunk), bf16),
        ((R, K), bf16),
        ((X, R, K), bf16),
        ((chunk, K), f32),
        ((chunk // Y, K), bf16),
        ((chunk // Y, K), bf16),
        ((Z, own, K), bf16),
        ((Z, own, K), bf16),
        ((C, 2 * K), f32),
        ((X * Y, block_rows, 2 * K), bf16),
        ((X * Y, block_rows, 2 * K), bf16),
        ((block_rows, 2 * K), bf16),
        ((Z, block_rows, 2 * K), bf16),
        ((X * Y, block_rows, 2 * K), bf16),
    ]
    sum_down, sum_up, sum_gain = pl.pallas_call(
        functools.partial(kernel, (X, Y, Z)),
        out_shape=(
            jax.ShapeDtypeStruct((own, K), f32),
            jax.ShapeDtypeStruct((own, K), f32),
            jax.ShapeDtypeStruct((1, own), f32),
        ),
        in_specs=[any_space] * 4 + [vmem] * 2,
        out_specs=(vmem, vmem, vmem),
        scratch_shapes=[pltpu.VMEM(shape, kind) for shape, kind in scratch]
        + [
            pltpu.SemaphoreType.DMA((3,)),
            pltpu.SemaphoreType.DMA((160,)),
            pltpu.SemaphoreType.DMA((recv_count,)),
        ],
        compiler_params=pltpu.CompilerParams(
            collective_id=0, has_side_effects=True, vmem_limit_bytes=56 * 1024 * 1024
        ),
    )(hidden_in, head_grad, down_w[0, 0], up_w[0, 0], norm_gain[0], codec)
    return (sum_down[None, None], sum_up[None, None], sum_gain[None])


def solution(mesh):
    in_specs = (
        P(None, "dp", None),
        P(None, "dp", None),
        P("section", None, None, None),
        P("section", None, None, None),
        P("section", None, None),
        P("dp", None),
    )
    out_specs = (
        P("section", None, "dp", None),
        P("section", None, "dp", None),
        P("section", None, "dp"),
    )
    return jax.shard_map(
        on_device, mesh=mesh, in_specs=in_specs, out_specs=out_specs, check_vma=False
    )
```

time: 1140 us -> 96.7 us (0.08)
  the two profiles are of different devices: /device:TPU:16 before, /device:TPU:1 now
where the time goes in v1:
time: 96.7 us; the launch traced here: 96.4 us
  Pallas kernels  91.7 us (95%)
  local copies, waits for them, and re-layouts  4.07 us (4%)
    pallas_call x1, Pallas kernels, on_device(): pl.pallas_call(functools.partial(kernel, (X, Y, Z)), out_shape=(jax.Shape...  91.7 us
    unnamed x3, local copies, waits for them, and re-layouts  4.07 us

profile of v1, /device:TPU:1, one launch (start us, length us, event | category | flops | bytes accessed | tf_op | source)
XLA Modules:
  0.0 96.4 jit_solution(11427757734010125706)
XLA Ops:
  0.6 91.7 %shard_map.85 = (f32[56,256]{1,0:T(8,128)}, f32[56,256]{1,0:T(8,128)}, f32[1,56]{1,0:T(1,128)}) custom-call(bf16[2,64,3584]{2,1,0:T(8,128)(2,1)} %hidden.1, bf16[2,64,3584]{2,1,0:T(8,128)(2,1)} %head.1, bf16[3584,256]{1,0:T(8,128)(2,1)} %bitcast.6, bf16[3584,256]{1,0:T(8,128)(2,1)} %bitcast.7, f32[1,3584]{1,0:T(1,128)} %bitcast.10, bf16[56,512]{1,0:T(8,128)(2,1)} %codec.1), custom_call_target="tpu_custom_call" | custom-call | tf_op jit(solution)/shard_map/pallas_call | solution.py:561
  92.4 1.4 %copy.12 = f32[1,1,56,256]{3,2,1,0:T(8,128)} copy(f32[1,1,56,256]{3,2,1,0:T(8,128)} %bitcast.9) | data formatting | bytes 114688
  93.8 1.4 %copy.13 = f32[1,1,56,256]{3,2,1,0:T(8,128)} copy(f32[1,1,56,256]{3,2,1,0:T(8,128)} %bitcast.8) | data formatting | bytes 114688
  95.3 1.2 %copy.14 = f32[1,1,56]{2,1,0:T(1,128)} copy(f32[1,1,56]{2,1,0:T(1,128)} %bitcast.11) | data formatting | bytes 448

commit v2 on v1

v2 whole, which is shorter than its diff:
```python
import functools

import jax
import jax.numpy as jnp
from jax import lax
from jax.experimental import pallas as pl
from jax.experimental.pallas import tpu as pltpu
from jax.sharding import PartitionSpec as P

epsilon = 1e-06
y_size, z_size = 2, 8
f32, bf16 = jnp.float32, jnp.bfloat16
mesh_ids = pl.DeviceIdType.MESH


def plain_dot(left, right):
    return lax.dot_general(left, right, (((1,), (0,)), ((), ())), preferred_element_type=f32)


def right_dot(left, right):
    return lax.dot_general(left, right, (((1,), (1,)), ((), ())), preferred_element_type=f32)


def left_dot(left, right):
    return lax.dot_general(left, right, (((0,), (0,)), ((), ())), preferred_element_type=f32)


def sigmoid(value):
    return 1.0 / (1.0 + jnp.exp(-value))


def silu_slope(latent):
    gate = sigmoid(latent)
    return gate * (1.0 + latent * (1.0 - gate))


def kernel(
    sizes,
    hidden,
    head,
    down_hbm,
    up_hbm,
    gain,
    codec,
    out_down,
    out_up,
    out_gain,
    tok,
    down,
    up,
    down32,
    gain_col,
    gdown,
    planes,
    flat,
    tok_half,
    acc,
    weights,
    tok_code,
    latent_ref,
    active_ref,
    inv_ref,
    slope_ref,
    code_grid,
    code_in,
    code_out,
    back_in,
    back_out,
    active_in,
    wide_in,
    factor,
    factor_in,
    wide_part,
    wide_parts,
    wide_sum,
    down_part,
    down_in,
    down_block,
    down_blocks,
    down_sum,
    up_part,
    up_parts,
    up_line,
    up_lines,
    up_sum,
    up_result,
    up_results,
    local_sem,
    send_sem,
    recv_sem,
):
    X, Y, Z = sizes
    micro, rows, D = hidden.shape
    R = micro * rows
    C, K = codec.shape[1], down.shape[1]
    own = codec.shape[0]
    lanes = C // 4
    chunk = D // X
    ratio = D / C
    sec = lax.axis_index("section")
    dp = lax.axis_index("dp")
    core = lax.rem(sec, 2)
    x = dp // (Y * Z)
    y = lax.rem(dp // Z, Y)
    z = lax.rem(dp, Z)
    xy = dp // Z
    other_y = 1 - y
    far_sec = lax.rem(sec + 2, 4)
    sibling = sec + 1 - 2 * core
    ends = jnp.logical_or(sec == 0, sec == 3)
    middle = jnp.logical_not(ends)

    def place(px, py, pz):
        return (px * Y + py) * Z + pz

    def ring(mine, count):
        return [lax.rem(mine + off, count) for off in range(1, count)]

    def near_first(mine, count):
        offsets = sorted(range(1, count), key=lambda off: (min(off, count - off), off))
        return [lax.rem(mine + off, count) for off in offsets]

    names = [
        ("x0", X), ("z0", Z), ("y0", Z), ("z1", Z), ("y1", 2), ("x1a", X), ("x1b", X),
        ("d0", 2), ("d1a", X), ("d1b", X), ("code", 1), ("back", 1), ("active", 1), ("up", 1),
        ("wide", X * Y), ("factor", X * Y), ("big", Z), ("down_a", Z), ("down_b", X * Y),
        ("down_c", Z), ("up_a", X * Y), ("up_b", Z), ("up_c", X * Y),
    ]
    base, total = {}, 0
    for name, count in names:
        base[name] = total
        total += count
    sent = [0]

    def start(src, dst, name, index, section, place_at, slot=None):
        if slot is None:
            slot = sent[0]
            sent[0] += 1
        copy = pltpu.make_async_remote_copy(
            src_ref=src, dst_ref=dst, send_sem=send_sem.at[slot],
            recv_sem=recv_sem.at[base[name] + index],
            device_id=(section, place_at), device_id_type=mesh_ids,
        )
        copy.start()
        return copy

    def left(src, slot):
        pltpu.make_async_remote_copy(
            src_ref=src, dst_ref=src, send_sem=send_sem.at[slot], recv_sem=recv_sem.at[0],
            device_id=(sec, dp), device_id_type=mesh_ids,
        ).wait_send()

    def arrive(dst, name, index):
        pltpu.make_async_remote_copy(
            src_ref=dst, dst_ref=dst, send_sem=send_sem.at[0],
            recv_sem=recv_sem.at[base[name] + index],
            device_id=(sec, dp), device_id_type=mesh_ids,
        ).wait_recv()

    load_down = pltpu.make_async_copy(down_hbm, down, local_sem.at[0])
    load_up = pltpu.make_async_copy(up_hbm, up, local_sem.at[1])
    load_hidden = pltpu.make_async_copy(hidden, tok, local_sem.at[2])
    load_head = pltpu.make_async_copy(head, tok, local_sem.at[2])
    load_down.start()
    load_up.start()
    pl.when(sec == 0)(load_hidden.start)
    pl.when(sec == 3)(load_head.start)

    color0, color1 = 2 * core, 2 * core + 1

    @pl.when(core == 0)
    def _():
        planes[0, x, y, z] = codec[:, 0:lanes]
        planes[1, x, y, z] = codec[:, lanes : 2 * lanes]

    @pl.when(core == 1)
    def _():
        planes[2, x, y, z] = codec[:, 2 * lanes : 3 * lanes]
        planes[3, x, y, z] = codec[:, 3 * lanes :]

    barrier = pltpu.get_barrier_semaphore()
    peers = [(sec, place(x, y, pz)) for pz in ring(z, Z)]
    xy_ring = ring(xy, X * Y)
    peers += [(sec, pxy * Z + z) for pxy in xy_ring]
    peers += [(sibling, dp), (far_sec, place(x, other_y, z)), (3 - sec, dp)]
    for peer in peers:
        pl.semaphore_signal(barrier, inc=1, device_id=peer, device_id_type=mesh_ids)
    pl.semaphore_wait(barrier, len(peers))

    half_z = Z // 2
    copies = []
    mine = planes.at[color0, x, y, z]
    for px in ring(x, X):
        copies.append(start(mine, mine, "x0", x, sec, place(px, y, z)))
    mine = planes.at[color1, x, y, z]
    for pz in near_first(z, Z):
        copies.append(start(mine, mine, "z1", z, sec, place(x, y, pz)))

    y_part = chunk // Y

    @pl.when(sec == 0)
    def _():
        load_hidden.wait()

    @pl.when(sec == 3)
    def _():
        load_head.wait()

    @pl.when(ends)
    def _():
        def split(index, carry):
            at = pl.ds(pl.multiple_of(index * chunk, chunk), chunk)
            value = tok[:, :, at].reshape(R, chunk)
            for py in range(Y):
                tok_half[py, index] = value[:, py * y_part : (py + 1) * y_part]
            return carry

        lax.fori_loop(0, X, split, 0)

    for px in ring(x, X):
        arrive(planes.at[color0, px, y, z], "x0", px)

    def line(pz):
        return planes.at[color0, :, y, pz]

    def pass_y(index, pz):
        block = line(pz)
        section = sec if index % 2 == 0 else far_sec
        copies.append(start(block, block, "y0", pz, section, place(x, other_y, z)))

    for pz in near_first(z, Z):
        copies.append(start(line(z), line(z), "z0", z, sec, place(x, y, pz)))
    pass_y(0, z)

    load_down.wait()
    load_up.wait()

    @pl.when(sec == 0)
    def _():
        def squares(index, carry):
            at = pl.ds(pl.multiple_of(index * chunk, chunk), chunk)
            value = tok[:, :, at].reshape(R, chunk).astype(f32)
            return carry + jnp.sum(value * value, axis=-1, keepdims=True)

        square = lax.fori_loop(0, X, squares, jnp.zeros((R, 1), f32))
        inverse = lax.rsqrt(square / D + epsilon)
        inv_ref[...] = inverse

        def project(index, carry):
            at = pl.ds(pl.multiple_of(index * chunk, chunk), chunk)
            value = tok[:, :, at].reshape(R, chunk).astype(f32)
            normed = (value * inverse * gain[:, at]).astype(bf16)
            return carry + plain_dot(normed, down[at, :])

        latent = lax.fori_loop(0, X, project, jnp.zeros((R, K), f32))
        active_ref[...] = (latent * sigmoid(latent)).astype(bf16)
        slope_ref[...] = silu_slope(latent)

    @pl.when(sec == 3)
    def _():
        def project(index, carry):
            at = pl.ds(pl.multiple_of(index * chunk, chunk), chunk)
            return carry + plain_dot(tok[:, :, at].reshape(R, chunk), up[at, :])

        latent_ref[...] = lax.fori_loop(0, X, project, jnp.zeros((R, K), f32))

    for pz in ring(z, Z):
        arrive(planes.at[color1, x, y, pz], "z1", pz)
    near, far = planes.at[color1, x, y, 0:half_z], planes.at[color1, x, y, half_z:Z]
    copies.append(start(near, near, "y1", 0, sec, place(x, other_y, z)))
    copies.append(start(far, far, "y1", 1, far_sec, place(x, other_y, z)))
    slab = planes.at[color1, x, y]
    for px in ring(x, X):
        copies.append(start(slab, slab, "x1a", x, sec, place(px, y, z)))
    copies.append(start(slab, slab, "d1a", x, sibling, dp))

    step = 128

    def scale_rows(index, carry):
        at = pl.ds(pl.multiple_of(index * step, step), step)
        column = jnp.broadcast_to(gain[:, at], (step, step)).T
        gain_col[at, :] = column
        wide = down[at, :].astype(f32)
        down32[at, :] = wide
        parts = [wide[:, k : k + step] * column[:, : min(step, K)] for k in range(0, K, step)]
        gdown[at, :] = jnp.concatenate(parts, axis=1).astype(bf16)
        return carry

    def scale():
        lax.fori_loop(0, D // step, scale_rows, 0)

    pl.when(sec != 0)(scale)

    order = near_first(z, Z)
    for index, pz in enumerate(order):
        if index == 2:
            arrive(planes.at[color1, x, other_y, 0:half_z], "y1", 0)
            arrive(planes.at[color1, x, other_y, half_z:Z], "y1", 1)
            slab = planes.at[color1, x, other_y]
            for px in ring(x, X):
                copies.append(start(slab, slab, "x1b", x, sec, place(px, y, z)))
            copies.append(start(slab, slab, "d1b", x, sibling, dp))
        arrive(line(pz), "z0", pz)
        pass_y(index + 1, pz)
    half = planes.at[color0, :, y]
    copies.append(start(half, half, "d0", 0, sibling, dp))
    for px in ring(x, X):
        slab = planes.at[color1, px, y]
        arrive(slab, "x1a", px)
        copies.append(start(slab, slab, "d1a", px, sibling, dp))

    their0, their1 = 2 - 2 * core, 3 - 2 * core
    acc[...] = jnp.zeros_like(acc)

    @pl.when(ends)
    def _():
        tok_code[...] = jnp.zeros_like(tok_code)

    def products(py):
        def body(index, carry):
            at = pl.ds(pl.multiple_of(index * chunk + py * y_part, y_part), y_part)
            for color in range(4):
                piece = planes[color, index, py].astype(f32).reshape(y_part, lanes).astype(bf16)
                flat[:, color * lanes : (color + 1) * lanes] = piece
            block = flat[...]

            @pl.when(sec != 3)
            def _():
                acc[:, K + C :] += left_dot(block, up[at, :])

            @pl.when(sec != 0)
            def _():
                acc[:, 0:K] += left_dot(block, gdown[at, :])
                acc[:, K : K + C] += left_dot(block, block)

            @pl.when(ends)
            def _():
                tok_code[...] += plain_dot(tok_half[py, index], block)

            return carry

        lax.fori_loop(0, X, body, 0)

    arrive(planes.at[their0, :, y], "d0", 0)
    arrive(planes.at[their1, x, y], "d1a", x)
    for px in ring(x, X):
        arrive(planes.at[their1, px, y], "d1a", px)
    products(y)

    for index, pz in enumerate([z] + order):
        arrive(planes.at[color0, :, other_y, pz], "y0", pz)
    half = planes.at[color0, :, other_y]
    copies.append(start(half, half, "d0", 1, sibling, dp))
    for px in ring(x, X):
        slab = planes.at[color1, px, other_y]
        arrive(slab, "x1b", px)
        copies.append(start(slab, slab, "d1b", px, sibling, dp))

    arrive(planes.at[their0, :, other_y], "d0", 1)
    arrive(planes.at[their1, x, other_y], "d1b", x)
    for px in ring(x, X):
        arrive(planes.at[their1, px, other_y], "d1b", px)

    wide_slot = sent[0]
    sent[0] += X * Y - 1

    @pl.when(ends)
    def _():
        for off, pxy in enumerate(xy_ring):
            start(
                tok_half.at[lax.rem(pxy, Y), pxy // Y], wide_in.at[xy], "wide", xy, sec,
                pxy * Z + z, wide_slot + off,
            )

    products(other_y)
    weights[...] = acc[...].astype(bf16)

    def forward():
        code = code_in[...]
        both = plain_dot(code, weights[:, 0 : K + C])
        grid = both[:, K:]
        square = jnp.sum(code.astype(f32) * grid, axis=-1, keepdims=True) * (ratio * ratio / D)
        inverse = lax.rsqrt(square + epsilon)
        latent = ratio * inverse * both[:, 0:K]
        active = (latent * sigmoid(latent)).astype(bf16)
        return code, grid, inverse, latent, active

    def backward(inner, grid, inverse, latent, d_latent):
        weight = jnp.sum(d_latent.astype(f32) * latent, axis=-1, keepdims=True)
        weight = weight * inverse * inverse * (ratio / D)
        through = right_dot(d_latent, weights[:, 0:K])
        return (ratio * (inner + inverse * through - weight * grid)).astype(bf16)

    def hop_active():
        return start(active_ref, active_in, "active", 0, sec + 1, dp)

    @pl.when(sec == 0)
    def _():
        result = tok_code[...] + right_dot(active_ref[...], weights[:, K + C :])
        code_out[...] = result.astype(bf16)
        hop = start(code_out, code_in, "code", 0, 1, dp)
        more = hop_active()
        hop.wait_send()
        more.wait_send()

    @pl.when(middle)
    def _():
        arrive(code_in, "code", 0)
        code, grid, inverse, latent, active = forward()
        result = ratio * grid + right_dot(active, weights[:, K + C :])
        code_out[...] = result.astype(bf16)
        hop = start(code_out, code_in, "code", 0, sec + 1, dp)
        active_ref[...] = active
        more = hop_active()
        code_grid[...] = grid
        inv_ref[...] = inverse
        latent_ref[...] = latent
        slope_ref[...] = silu_slope(latent)
        hop.wait_send()
        more.wait_send()

    def code_sums(code, inverse, d_latent):
        scaled = (d_latent.astype(f32) * (ratio * inverse)).astype(bf16)
        down_part[...] = left_dot(code, scaled).astype(bf16).reshape(down_part.shape)

    @pl.when(sec == 3)
    def _():
        arrive(code_in, "code", 0)
        code, grid, inverse, latent, active = forward()
        factor[...] = active
        d_latent = (latent_ref[...] * silu_slope(latent)).astype(bf16)
        back_out[...] = backward(tok_code[...], grid, inverse, latent, d_latent)
        hop = start(back_out, back_in, "back", 0, 2, dp)
        code_sums(code, inverse, d_latent)
        hop.wait_send()

    @pl.when(middle)
    def _():
        arrive(back_in, "back", 0)
        both = plain_dot(back_in[...], weights[:, K:])
        inverse = inv_ref[...]
        d_latent = (both[:, C:] * slope_ref[...]).astype(bf16)
        back_out[...] = backward(both[:, 0:C], code_grid[...], inverse, latent_ref[...], d_latent)
        hop = start(back_out, back_in, "back", 0, sec - 1, dp)
        code_sums(code_in[...], inverse, d_latent)
        hop.wait_send()

    @pl.when(sec == 0)
    def _():
        scale()
        arrive(back_in, "back", 0)
        d_latent = (plain_dot(back_in[...], weights[:, K + C :]) * slope_ref[...]).astype(bf16)
        factor[...] = (d_latent.astype(f32) * inv_ref[...]).astype(bf16)

    XY = X * Y
    xy_peers = [(pxy, pxy * Z + z) for pxy in xy_ring]
    z_peers = [(pz, place(x, y, pz)) for pz in near_first(z, Z)]
    pending_rest, pending_ends = [], []

    def spread(ref_of, landings, name, mine, peers, pending):
        for peer, peer_dp in peers:
            slot = sent[0]
            start(ref_of(peer), landings.at[mine], name, mine, sec, peer_dp)
            pending.append((landings, slot))

    def gathered(first, landing, name, peers):
        value = first.astype(f32)
        for peer, _ in peers:
            arrive(landing.at[peer], name, peer)
            value = value + landing[peer].astype(f32)
        return value

    rest = sec != 0

    @pl.when(rest)
    def _():
        spread(lambda peer: down_part.at[peer], down_in, "down_a", z, z_peers, pending_rest)
        arrive(active_in, "active", 0)
        up_part[...] = left_dot(back_out[...], active_in[...]).astype(bf16).reshape(up_part.shape)
        spread(lambda peer: up_part.at[peer], up_parts, "up_a", xy, xy_peers, pending_rest)

    @pl.when(ends)
    def _():
        spread(lambda peer: factor, factor_in, "factor", xy, xy_peers, pending_ends)

    @pl.when(rest)
    def _():
        up_line[...] = gathered(up_part[xy], up_parts, "up_a", xy_peers).astype(bf16)
        spread(lambda peer: up_line, up_lines, "up_b", z, z_peers, pending_rest)

    @pl.when(ends)
    def _():
        value = left_dot(tok_half[y, x], factor[...])
        for pxy, _ in xy_peers:
            arrive(wide_in.at[pxy], "wide", pxy)
            arrive(factor_in.at[pxy], "factor", pxy)
            value = value + left_dot(wide_in[pxy], factor_in[pxy])
        wide_part[...] = value.reshape(Z, own, K).astype(bf16)
        spread(lambda peer: wide_part.at[peer], wide_parts, "big", z, z_peers, pending_ends)

    @pl.when(rest)
    def _():
        down_block[...] = gathered(down_part[z], down_in, "down_a", z_peers).astype(bf16)
        spread(lambda peer: down_block, down_blocks, "down_b", xy, xy_peers, pending_rest)
        up_sum[xy] = gathered(up_line[...], up_lines, "up_b", z_peers).astype(bf16)
        spread(lambda peer: up_sum.at[xy], up_sum, "up_c", xy, xy_peers, pending_rest)
        down_sum[z] = gathered(down_block[...], down_blocks, "down_b", xy_peers).astype(bf16)
        spread(lambda peer: down_sum.at[z], down_sum, "down_c", z, z_peers, pending_rest)
        for pxy, _ in xy_peers:
            arrive(up_sum.at[pxy], "up_c", pxy)
        up_result[...] = plain_dot(codec[...], up_sum[...].reshape(C, K))
        hop = start(up_result, up_results, "up", 0, sec - 1, dp)
        hop.wait_send()

    own_rows = pl.ds(pl.multiple_of(dp * own, 8), own)

    def put_down(value):
        column = gain_col[own_rows, :]
        weighted = down32[own_rows, :] * value
        folded = weighted[:, 0 : min(step, K)]
        for k in range(step, K, step):
            folded = folded + weighted[:, k : k + step]
        if own < step:
            folded = jnp.concatenate([folded, jnp.zeros((step - own, folded.shape[1]), f32)], axis=0)
        out_gain[...] = jnp.sum(folded.T, axis=0, keepdims=True)[:, 0:own]
        for k in range(0, K, step):
            out_down[:, k : k + step] = value[:, k : k + step] * column[:, : min(step, K)]

    @pl.when(ends)
    def _():
        wide_sum[...] = gathered(wide_part[z], wide_parts, "big", z_peers)

    @pl.when(rest)
    def _():
        for pz, _ in z_peers:
            arrive(down_sum.at[pz], "down_c", pz)
        put_down(plain_dot(codec[...], down_sum[...].reshape(C, K)))

    @pl.when(sec == 0)
    def _():
        put_down(wide_sum[...])

    @pl.when(sec == 3)
    def _():
        out_up[...] = wide_sum[...]

    @pl.when(sec != 3)
    def _():
        arrive(up_results, "up", 0)
        out_up[...] = up_results[...]

    @pl.when(rest)
    def _():
        for landing, slot in pending_rest:
            left(landing.at[0], slot)

    @pl.when(ends)
    def _():
        for landing, slot in pending_ends:
            left(landing.at[0], slot)
        for off in range(XY - 1):
            left(wide_in.at[0], wide_slot + off)

    for copy in copies:
        copy.wait_send()


def hand_out(down, up, gain, out_down, out_up, out_gain):
    out_down[...] = down[...]
    out_up[...] = up[...]
    out_gain[...] = gain[...]


def on_device(hidden_in, head_grad, down_w, up_w, norm_gain, codec):
    micro, rows, D = hidden_in.shape
    K, C, own = down_w.shape[3], codec.shape[1], codec.shape[0]
    Y, Z = y_size, z_size
    X = lax.axis_size("dp") // (Y * Z)
    R, chunk, lanes = micro * rows, D // X, C // 4
    block_rows = C // (X * Y)
    any_space = pl.BlockSpec(memory_space=pl.ANY)
    vmem = pl.BlockSpec(memory_space=pltpu.VMEM)
    recv_count = 5 * X + 7 * Z + 8 + 5 * X * Y
    scratch = [
        ((micro, rows, D), bf16),
        ((D, K), bf16),
        ((D, K), bf16),
        ((D, K), f32),
        ((D, 128), f32),
        ((D, K), bf16),
        ((4, X, Y, Z, own, lanes), bf16),
        ((chunk // Y, C), bf16),
        ((Y, X, R, chunk // Y), bf16),
        ((C, 2 * K + C), f32),
        ((C, 2 * K + C), bf16),
        ((R, C), f32),
        ((R, K), f32),
        ((R, K), bf16),
        ((R, 1), f32),
        ((R, K), f32),
        ((R, C), f32),
        ((R, C), bf16),
        ((R, C), bf16),
        ((R, C), bf16),
        ((R, C), bf16),
        ((R, K), bf16),
        ((X * Y, R, chunk // Y), bf16),
        ((R, K), bf16),
        ((X * Y, R, K), bf16),
        ((Z, own, K), bf16),
        ((Z, own, K), bf16),
        ((own, K), f32),
        ((Z, C // Z, K), bf16),
        ((Z, C // Z, K), bf16),
        ((C // Z, K), bf16),
        ((X * Y, C // Z, K), bf16),
        ((Z, C // Z, K), bf16),
        ((X * Y, block_rows, K), bf16),
        ((X * Y, block_rows, K), bf16),
        ((block_rows, K), bf16),
        ((Z, block_rows, K), bf16),
        ((X * Y, block_rows, K), bf16),
        ((own, K), f32),
        ((own, K), f32),
    ]
    sum_down, sum_up, sum_gain = pl.pallas_call(
        functools.partial(kernel, (X, Y, Z)),
        out_shape=(
            jax.ShapeDtypeStruct((own, K), f32),
            jax.ShapeDtypeStruct((own, K), f32),
            jax.ShapeDtypeStruct((1, own), f32),
        ),
        in_specs=[any_space] * 4 + [vmem] * 2,
        out_specs=(vmem, vmem, vmem),
        scratch_shapes=[pltpu.VMEM(shape, kind) for shape, kind in scratch]
        + [
            pltpu.SemaphoreType.DMA((3,)),
            pltpu.SemaphoreType.DMA((160,)),
            pltpu.SemaphoreType.DMA((recv_count,)),
        ],
        compiler_params=pltpu.CompilerParams(
            collective_id=0, has_side_effects=True, vmem_limit_bytes=56 * 1024 * 1024
        ),
    )(hidden_in, head_grad, down_w[0, 0], up_w[0, 0], norm_gain[0], codec)
    sum_down, sum_up, sum_gain = pl.pallas_call(
        hand_out,
        out_shape=(
            jax.ShapeDtypeStruct((own, K), f32),
            jax.ShapeDtypeStruct((own, K), f32),
            jax.ShapeDtypeStruct((1, own), f32),
        ),
        in_specs=[vmem] * 3,
        out_specs=(vmem, vmem, vmem),
    )(sum_down, sum_up, sum_gain)
    return (sum_down[None, None], sum_up[None, None], sum_gain[None])


def solution(mesh):
    in_specs = (
        P(None, "dp", None),
        P(None, "dp", None),
        P("section", None, None, None),
        P("section", None, None, None),
        P("section", None, None),
        P("dp", None),
    )
    out_specs = (
        P("section", None, "dp", None),
        P("section", None, "dp", None),
        P("section", None, "dp"),
    )
    return jax.shard_map(
        on_device, mesh=mesh, in_specs=in_specs, out_specs=out_specs, check_vma=False
    )
```

time: 96.7 us -> 85.1 us (0.88)
  Pallas kernels: 91.7 us -> 84.3 us
  local copies, waits for them, and re-layouts: 4.07 us -> 0 us
    pallas_call x1, Pallas kernels: 91.7 us -> 82.8 us  [on_device(): pl.pallas_call(functools.partial(kernel, (X, Y, Z)), out_shape=(jax.Shape...]
    unnamed x3 -> x0, local copies, waits for them, and re-layouts: 4.07 us -> none
    pallas_call x0 -> x1, Pallas kernels: none -> 1.5 us  [on_device(): pl.pallas_call(hand_out, out_shape=(jax.ShapeDtypeStruct((own, K), f32),...]
where the time goes in v2:
time: 85.1 us; the launch traced here: 84.9 us
  Pallas kernels  84.3 us (99%)
    pallas_call x1, Pallas kernels, on_device(): pl.pallas_call(functools.partial(kernel, (X, Y, Z)), out_shape=(jax.Shape...  82.8 us

profile of v2, /device:TPU:1, one launch (start us, length us, event | category | flops | bytes accessed | tf_op | source)
XLA Modules:
  0.0 84.9 jit_solution(2255403564017386049)
XLA Ops:
  0.6 82.8 %shard_map.85 = (f32[56,256]{1,0:T(8,128)}, f32[56,256]{1,0:T(8,128)}, f32[1,56]{1,0:T(1,128)}) custom-call(bf16[2,64,3584]{2,1,0:T(8,128)(2,1)} %hidden.1, bf16[2,64,3584]{2,1,0:T(8,128)(2,1)} %head.1, bf16[3584,256]{1,0:T(8,128)(2,1)} %bitcast.6, bf16[3584,256]{1,0:T(8,128)(2,1)} %bitcast.7, f32[1,3584]{1,0:T(1,128)} %bitcast.8, bf16[56,512]{1,0:T(8,128)(2,1)} %codec.1), custom_call_target="tpu_custom_call" | custom-call | tf_op jit(solution)/shard_map/pallas_call | solution.py:626
  83.4 1.5 %shard_map.86 = (f32[56,256]{1,0:T(8,128)}, f32[56,256]{1,0:T(8,128)}, f32[1,56]{1,0:T(1,128)}) custom-call(f32[56,256]{1,0:T(8,128)} %get-tuple-element.9.down, f32[56,256]{1,0:T(8,128)} %get-tuple-element.10.up, f32[1,56]{1,0:T(1,128)} %get-tuple-element.11.gain), custom_call_target="tpu_custom_call" | custom-call | tf_op jit(solution)/shard_map/pallas_call | solution.py:645

commit v3 on v2

--- a/solution.py
+++ b/solution.py
@@ -40,17 +40,19 @@
     head,
     down_hbm,
     up_hbm,
-    gain,
-    codec,
+    gain_hbm,
+    codec_hbm,
     out_down,
     out_up,
     out_gain,
     tok,
+    gain,
+    codec,
     down,
-    up,
+    up_half,
     down32,
     gain_col,
-    gdown,
+    gdown_half,
     planes,
     flat,
     tok_half,
@@ -94,6 +96,7 @@
     R = micro * rows
     C, K = codec.shape[1], down.shape[1]
     own = codec.shape[0]
+    y_part = D // (X * Y)
     lanes = C // 4
     chunk = D // X
     ratio = D / C
@@ -157,27 +160,6 @@
             device_id=(sec, dp), device_id_type=mesh_ids,
         ).wait_recv()
 
-    load_down = pltpu.make_async_copy(down_hbm, down, local_sem.at[0])
-    load_up = pltpu.make_async_copy(up_hbm, up, local_sem.at[1])
-    load_hidden = pltpu.make_async_copy(hidden, tok, local_sem.at[2])
-    load_head = pltpu.make_async_copy(head, tok, local_sem.at[2])
-    load_down.start()
-    load_up.start()
-    pl.when(sec == 0)(load_hidden.start)
-    pl.when(sec == 3)(load_head.start)
-
-    color0, color1 = 2 * core, 2 * core + 1
-
-    @pl.when(core == 0)
-    def _():
-        planes[0, x, y, z] = codec[:, 0:lanes]
-        planes[1, x, y, z] = codec[:, lanes : 2 * lanes]
-
-    @pl.when(core == 1)
-    def _():
-        planes[2, x, y, z] = codec[:, 2 * lanes : 3 * lanes]
-        planes[3, x, y, z] = codec[:, 3 * lanes :]
-
     barrier = pltpu.get_barrier_semaphore()
     peers = [(sec, place(x, y, pz)) for pz in ring(z, Z)]
     xy_ring = ring(xy, X * Y)
@@ -185,7 +167,38 @@
     peers += [(sibling, dp), (far_sec, place(x, other_y, z)), (3 - sec, dp)]
     for peer in peers:
         pl.semaphore_signal(barrier, inc=1, device_id=peer, device_id_type=mesh_ids)
+
+    color0, color1 = 2 * core, 2 * core + 1
+    loads = []
+
+    def load(src, dst):
+        copy = pltpu.make_async_copy(src, dst, local_sem.at[len(loads)])
+        loads.append(copy)
+        copy.start()
+        return copy
+
+    own_loads = []
+    for color in (color0, color1):
+        columns = pl.ds(pl.multiple_of(color * lanes, lanes), lanes)
+        own_loads.append(load(codec_hbm.at[:, columns], planes.at[color, x, y, z]))
+    load_tok = pltpu.make_async_copy(hidden, tok, local_sem.at[20])
+    pl.when(sec == 0)(load_tok.start)
+    pl.when(sec == 3)(pltpu.make_async_copy(head, tok, local_sem.at[20]).start)
+    load_down = load(down_hbm, down)
+    load_ups = [
+        load(
+            up_hbm.at[pl.ds(index * chunk + py * y_part, y_part)],
+            up_half.at[py, pl.ds(index * y_part, y_part)],
+        )
+        for py in range(Y)
+        for index in range(X)
+    ]
+    load_gain = load(gain_hbm, gain)
+    load_codec = load(codec_hbm, codec)
+
     pl.semaphore_wait(barrier, len(peers))
+    for copy in own_loads:
+        copy.wait()
 
     half_z = Z // 2
     copies = []
@@ -196,18 +209,13 @@
     for pz in near_first(z, Z):
         copies.append(start(mine, mine, "z1", z, sec, place(x, y, pz)))
 
-    y_part = chunk // Y
-
-    @pl.when(sec == 0)
-    def _():
-        load_hidden.wait()
-
-    @pl.when(sec == 3)
-    def _():
-        load_head.wait()
+    wide_slot = sent[0]
+    sent[0] += X * Y - 1
 
     @pl.when(ends)
     def _():
+        load_tok.wait()
+
         def split(index, carry):
             at = pl.ds(pl.multiple_of(index * chunk, chunk), chunk)
             value = tok[:, :, at].reshape(R, chunk)
@@ -216,6 +224,11 @@
             return carry
 
         lax.fori_loop(0, X, split, 0)
+        for off, pxy in enumerate(xy_ring):
+            start(
+                tok_half.at[lax.rem(pxy, Y), pxy // Y], wide_in.at[xy], "wide", xy, sec,
+                pxy * Z + z, wide_slot + off,
+            )
 
     for px in ring(x, X):
         arrive(planes.at[color0, px, y, z], "x0", px)
@@ -233,7 +246,9 @@
     pass_y(0, z)
 
     load_down.wait()
-    load_up.wait()
+    load_gain.wait()
+    for copy in load_ups:
+        copy.wait()
 
     @pl.when(sec == 0)
     def _():
@@ -258,11 +273,12 @@
 
     @pl.when(sec == 3)
     def _():
-        def project(index, carry):
-            at = pl.ds(pl.multiple_of(index * chunk, chunk), chunk)
-            return carry + plain_dot(tok[:, :, at].reshape(R, chunk), up[at, :])
-
-        latent_ref[...] = lax.fori_loop(0, X, project, jnp.zeros((R, K), f32))
+        value = jnp.zeros((R, K), f32)
+        for py in range(Y):
+            for index in range(X):
+                rows_at = pl.ds(index * y_part, y_part)
+                value = value + plain_dot(tok_half[py, index], up_half[py, rows_at, :])
+        latent_ref[...] = value
 
     for pz in ring(z, Z):
         arrive(planes.at[color1, x, y, pz], "z1", pz)
@@ -277,17 +293,20 @@
     step = 128
 
     def scale_rows(index, carry):
-        at = pl.ds(pl.multiple_of(index * step, step), step)
-        column = jnp.broadcast_to(gain[:, at], (step, step)).T
+        at = pl.ds(pl.multiple_of(index * chunk, chunk), chunk)
+        column = jnp.broadcast_to(gain[:, at], (step, chunk)).T
         gain_col[at, :] = column
         wide = down[at, :].astype(f32)
         down32[at, :] = wide
         parts = [wide[:, k : k + step] * column[:, : min(step, K)] for k in range(0, K, step)]
-        gdown[at, :] = jnp.concatenate(parts, axis=1).astype(bf16)
+        scaled = jnp.concatenate(parts, axis=1).astype(bf16)
+        rows_at = pl.ds(pl.multiple_of(index * y_part, y_part), y_part)
+        for py in range(Y):
+            gdown_half[py, rows_at, :] = scaled[py * y_part : (py + 1) * y_part]
         return carry
 
     def scale():
-        lax.fori_loop(0, D // step, scale_rows, 0)
+        lax.fori_loop(0, X, scale_rows, 0)
 
     pl.when(sec != 0)(scale)
 
@@ -310,42 +329,41 @@
         copies.append(start(slab, slab, "d1a", px, sibling, dp))
 
     their0, their1 = 2 - 2 * core, 3 - 2 * core
-    acc[...] = jnp.zeros_like(acc)
-
-    @pl.when(ends)
-    def _():
-        tok_code[...] = jnp.zeros_like(tok_code)
-
-    def products(py):
-        def body(index, carry):
-            at = pl.ds(pl.multiple_of(index * chunk + py * y_part, y_part), y_part)
+    def products(py, add):
+        for index in range(X):
             for color in range(4):
                 piece = planes[color, index, py].astype(f32).reshape(y_part, lanes).astype(bf16)
-                flat[:, color * lanes : (color + 1) * lanes] = piece
-            block = flat[...]
-
-            @pl.when(sec != 3)
-            def _():
-                acc[:, K + C :] += left_dot(block, up[at, :])
-
-            @pl.when(sec != 0)
-            def _():
-                acc[:, 0:K] += left_dot(block, gdown[at, :])
-                acc[:, K : K + C] += left_dot(block, block)
-
-            @pl.when(ends)
-            def _():
-                tok_code[...] += plain_dot(tok_half[py, index], block)
-
-            return carry
-
-        lax.fori_loop(0, X, body, 0)
+                rows_at = slice(index * y_part, (index + 1) * y_part)
+                flat[rows_at, color * lanes : (color + 1) * lanes] = piece
+
+        @pl.when(sec != 3)
+        def _():
+            add(acc, slice(K + C, K + C + K), left_dot(flat[...], up_half[py]))
+
+        @pl.when(ends)
+        def _():
+            value = jnp.zeros((R, C), f32)
+            for index in range(X):
+                rows_at = slice(index * y_part, (index + 1) * y_part)
+                value = value + plain_dot(tok_half[py, index], flat[rows_at, :])
+            add(tok_code, slice(0, C), value)
+
+        @pl.when(sec != 0)
+        def _():
+            add(acc, slice(0, K), left_dot(flat[...], gdown_half[py]))
+            add(acc, slice(K, K + C), left_dot(flat[...], flat[...]))
+
+    def put(ref, columns, value):
+        ref[:, columns] = value
+
+    def add_to(ref, columns, value):
+        ref[:, columns] += value
 
     arrive(planes.at[their0, :, y], "d0", 0)
     arrive(planes.at[their1, x, y], "d1a", x)
     for px in ring(x, X):
         arrive(planes.at[their1, px, y], "d1a", px)
-    products(y)
+    products(y, put)
 
     for index, pz in enumerate([z] + order):
         arrive(planes.at[color0, :, other_y, pz], "y0", pz)
@@ -361,19 +379,15 @@
     for px in ring(x, X):
         arrive(planes.at[their1, px, other_y], "d1b", px)
 
-    wide_slot = sent[0]
-    sent[0] += X * Y - 1
-
-    @pl.when(ends)
-    def _():
-        for off, pxy in enumerate(xy_ring):
-            start(
-                tok_half.at[lax.rem(pxy, Y), pxy // Y], wide_in.at[xy], "wide", xy, sec,
-                pxy * Z + z, wide_slot + off,
-            )
-
-    products(other_y)
-    weights[...] = acc[...].astype(bf16)
+    products(other_y, add_to)
+
+    @pl.when(sec != 3)
+    def _():
+        weights[:, K + C :] = acc[:, K + C :].astype(bf16)
+
+    @pl.when(sec != 0)
+    def _():
+        weights[:, 0 : K + C] = acc[:, 0 : K + C].astype(bf16)
 
     def forward():
         code = code_in[...]
@@ -391,17 +405,18 @@
         through = right_dot(d_latent, weights[:, 0:K])
         return (ratio * (inner + inverse * through - weight * grid)).astype(bf16)
 
-    def hop_active():
-        return start(active_ref, active_in, "active", 0, sec + 1, dp)
+    late = []
+
+    def hop(group, src, dst, name, section):
+        late.append((group, src, sent[0]))
+        start(src, dst, name, 0, section, dp)
 
     @pl.when(sec == 0)
     def _():
         result = tok_code[...] + right_dot(active_ref[...], weights[:, K + C :])
         code_out[...] = result.astype(bf16)
-        hop = start(code_out, code_in, "code", 0, 1, dp)
-        more = hop_active()
-        hop.wait_send()
-        more.wait_send()
+        hop("first", code_out, code_in, "code", 1)
+        hop("first", active_ref, active_in, "active", 1)
 
     @pl.when(middle)
     def _():
@@ -409,15 +424,13 @@
         code, grid, inverse, latent, active = forward()
         result = ratio * grid + right_dot(active, weights[:, K + C :])
         code_out[...] = result.astype(bf16)
-        hop = start(code_out, code_in, "code", 0, sec + 1, dp)
+        hop("middle", code_out, code_in, "code", sec + 1)
         active_ref[...] = active
-        more = hop_active()
+        hop("middle", active_ref, active_in, "active", sec + 1)
         code_grid[...] = grid
         inv_ref[...] = inverse
         latent_ref[...] = latent
         slope_ref[...] = silu_slope(latent)
-        hop.wait_send()
-        more.wait_send()
 
     def code_sums(code, inverse, d_latent):
         scaled = (d_latent.astype(f32) * (ratio * inverse)).astype(bf16)
@@ -430,9 +443,8 @@
         factor[...] = active
         d_latent = (latent_ref[...] * silu_slope(latent)).astype(bf16)
         back_out[...] = backward(tok_code[...], grid, inverse, latent, d_latent)
-        hop = start(back_out, back_in, "back", 0, 2, dp)
+        hop("last", back_out, back_in, "back", 2)
         code_sums(code, inverse, d_latent)
-        hop.wait_send()
 
     @pl.when(middle)
     def _():
@@ -441,9 +453,8 @@
         inverse = inv_ref[...]
         d_latent = (both[:, C:] * slope_ref[...]).astype(bf16)
         back_out[...] = backward(both[:, 0:C], code_grid[...], inverse, latent_ref[...], d_latent)
-        hop = start(back_out, back_in, "back", 0, sec - 1, dp)
+        hop("middle", back_out, back_in, "back", sec - 1)
         code_sums(code_in[...], inverse, d_latent)
-        hop.wait_send()
 
     @pl.when(sec == 0)
     def _():
@@ -471,6 +482,7 @@
         return value
 
     rest = sec != 0
+    load_codec.wait()
 
     @pl.when(rest)
     def _():
@@ -509,8 +521,7 @@
         for pxy, _ in xy_peers:
             arrive(up_sum.at[pxy], "up_c", pxy)
         up_result[...] = plain_dot(codec[...], up_sum[...].reshape(C, K))
-        hop = start(up_result, up_results, "up", 0, sec - 1, dp)
-        hop.wait_send()
+        hop("rest", up_result, up_results, "up", sec - 1)
 
     own_rows = pl.ds(pl.multiple_of(dp * own, 8), own)
 
@@ -561,14 +572,27 @@
         for off in range(XY - 1):
             left(wide_in.at[0], wide_slot + off)
 
+    for group, chosen in (("first", sec == 0), ("middle", middle), ("last", sec == 3), ("rest", rest)):
+        @pl.when(chosen)
+        def _():
+            for which, src, slot in late:
+                if which == group:
+                    left(src, slot)
+
     for copy in copies:
         copy.wait_send()
 
 
-def hand_out(down, up, gain, out_down, out_up, out_gain):
-    out_down[...] = down[...]
-    out_up[...] = up[...]
-    out_gain[...] = gain[...]
+def hand_out(down, up, gain, out_down, out_up, out_gain, sem):
+    copies = [
+        pltpu.make_async_copy(down, out_down, sem.at[0]),
+        pltpu.make_async_copy(up, out_up, sem.at[1]),
+        pltpu.make_async_copy(gain, out_gain, sem.at[2]),
+    ]
+    for copy in copies:
+        copy.start()
+    for copy in copies:
+        copy.wait()
 
 
 def on_device(hidden_in, head_grad, down_w, up_w, norm_gain, codec):
@@ -583,13 +607,15 @@
     recv_count = 5 * X + 7 * Z + 8 + 5 * X * Y
     scratch = [
         ((micro, rows, D), bf16),
+        ((1, D), f32),
+        ((own, C), bf16),
         ((D, K), bf16),
-        ((D, K), bf16),
+        ((Y, D // Y, K), bf16),
         ((D, K), f32),
         ((D, 128), f32),
-        ((D, K), bf16),
+        ((Y, D // Y, K), bf16),
         ((4, X, Y, Z, own, lanes), bf16),
-        ((chunk // Y, C), bf16),
+        ((D // Y, C), bf16),
         ((Y, X, R, chunk // Y), bf16),
         ((C, 2 * K + C), f32),
         ((C, 2 * K + C), bf16),
@@ -630,11 +656,11 @@
             jax.ShapeDtypeStruct((own, K), f32),
             jax.ShapeDtypeStruct((1, own), f32),
         ),
-        in_specs=[any_space] * 4 + [vmem] * 2,
+        in_specs=[any_space] * 6,
         out_specs=(vmem, vmem, vmem),
         scratch_shapes=[pltpu.VMEM(shape, kind) for shape, kind in scratch]
         + [
-            pltpu.SemaphoreType.DMA((3,)),
+            pltpu.SemaphoreType.DMA((21,)),
             pltpu.SemaphoreType.DMA((160,)),
             pltpu.SemaphoreType.DMA((recv_count,)),
         ],
@@ -649,8 +675,9 @@
             jax.ShapeDtypeStruct((own, K), f32),
             jax.ShapeDtypeStruct((1, own), f32),
         ),
-        in_specs=[vmem] * 3,
-        out_specs=(vmem, vmem, vmem),
+        in_specs=[any_space] * 3,
+        out_specs=(any_space,) * 3,
+        scratch_shapes=[pltpu.SemaphoreType.DMA((3,))],
     )(sum_down, sum_up, sum_gain)
     return (sum_down[None, None], sum_up[None, None], sum_gain[None])
 

time: 85.1 us -> 79.4 us (0.933)
  Pallas kernels: 84.3 us -> 78.7 us
    pallas_call x1, Pallas kernels: 82.8 us -> 74 us  [on_device(): pl.pallas_call(functools.partial(kernel, (X, Y, Z)), out_shape=(jax.Shape...]
    pallas_call x1, Pallas kernels: 1.5 us -> 4.62 us  [on_device(): pl.pallas_call(hand_out, out_shape=(jax.ShapeDtypeStruct((own, K), f32),...]
where the time goes in v3:
time: 79.4 us; the launch traced here: 79.3 us
  Pallas kernels  78.7 us (99%)
    pallas_call x1, Pallas kernels, on_device(): pl.pallas_call(functools.partial(kernel, (X, Y, Z)), out_shape=(jax.Shape...  74 us
    pallas_call x1, Pallas kernels, on_device(): pl.pallas_call(hand_out, out_shape=(jax.ShapeDtypeStruct((own, K), f32),...  4.62 us

profile of v3, /device:TPU:1, one launch (start us, length us, event | category | flops | bytes accessed | tf_op | source)
XLA Modules:
  0.0 79.3 jit_solution(9664708377890798358)
XLA Ops:
  0.6 74.0 %shard_map.85 = (f32[56,256]{1,0:T(8,128)}, f32[56,256]{1,0:T(8,128)}, f32[1,56]{1,0:T(1,128)}) custom-call(bf16[2,64,3584]{2,1,0:T(8,128)(2,1)} %hidden.1, bf16[2,64,3584]{2,1,0:T(8,128)(2,1)} %head.1, bf16[3584,256]{1,0:T(8,128)(2,1)} %bitcast.6, bf16[3584,256]{1,0:T(8,128)(2,1)} %bitcast.7, f32[1,3584]{1,0:T(1,128)} %bitcast.8, bf16[56,512]{1,0:T(8,128)(2,1)} %codec_hbm.1), custom_call_target="tpu_custom_call" | custom-call | tf_op jit(solution)/shard_map/pallas_call | solution.py:652
  74.7 4.6 %shard_map.86 = (f32[56,256]{1,0:T(8,128)}, f32[56,256]{1,0:T(8,128)}, f32[1,56]{1,0:T(1,128)}) custom-call(f32[56,256]{1,0:T(8,128)} %get-tuple-element.9.down, f32[56,256]{1,0:T(8,128)} %get-tuple-element.10.up, f32[1,56]{1,0:T(1,128)} %get-tuple-element.11.gain), custom_call_target="tpu_custom_call" | custom-call | tf_op jit(solution)/shard_map/pallas_call | solution.py:671

commit v4 on v3

--- a/solution.py
+++ b/solution.py
@@ -56,6 +56,7 @@
     planes,
     flat,
     tok_half,
+    out_half,
     acc,
     weights,
     tok_code,
@@ -63,11 +64,16 @@
     active_ref,
     inv_ref,
     slope_ref,
-    code_grid,
     code_in,
     code_out,
     back_in,
     back_out,
+    turn_out,
+    scaled_out,
+    scaled,
+    lead_weight,
+    lead_slope,
+    lead_code,
     active_in,
     wide_in,
     factor,
@@ -111,7 +117,6 @@
     far_sec = lax.rem(sec + 2, 4)
     sibling = sec + 1 - 2 * core
     ends = jnp.logical_or(sec == 0, sec == 3)
-    middle = jnp.logical_not(ends)
 
     def place(px, py, pz):
         return (px * Y + py) * Z + pz
@@ -125,7 +130,8 @@
 
     names = [
         ("x0", X), ("z0", Z), ("y0", Z), ("z1", Z), ("y1", 2), ("x1a", X), ("x1b", X),
-        ("d0", 2), ("d1a", X), ("d1b", X), ("code", 1), ("back", 1), ("active", 1), ("up", 1),
+        ("z4", 2), ("d0", 1), ("d0z", Z), ("d1a", X), ("d1b", X), ("code", 1), ("back", 1), ("active", 1), ("up", 1),
+        ("scaled", 1), ("lead_weight", 1), ("lead_slope", 1), ("lead_code", 1),
         ("wide", X * Y), ("factor", X * Y), ("big", Z), ("down_a", Z), ("down_b", X * Y),
         ("down_c", Z), ("up_a", X * Y), ("up_b", Z), ("up_c", X * Y),
     ]
@@ -163,7 +169,7 @@
     barrier = pltpu.get_barrier_semaphore()
     peers = [(sec, place(x, y, pz)) for pz in ring(z, Z)]
     xy_ring = ring(xy, X * Y)
-    peers += [(sec, pxy * Z + z) for pxy in xy_ring]
+    peers += [(which, pxy * Z + z) for which in (sec, sibling) for pxy in xy_ring]
     peers += [(sibling, dp), (far_sec, place(x, other_y, z)), (3 - sec, dp)]
     for peer in peers:
         pl.semaphore_signal(barrier, inc=1, device_id=peer, device_id_type=mesh_ids)
@@ -211,6 +217,7 @@
 
     wide_slot = sent[0]
     sent[0] += X * Y - 1
+    wide_peers = [(px, y) for px in ring(x, X)] + [(px, other_y) for px in [x] + ring(x, X)]
 
     @pl.when(ends)
     def _():
@@ -224,10 +231,10 @@
             return carry
 
         lax.fori_loop(0, X, split, 0)
-        for off, pxy in enumerate(xy_ring):
+        for off, (px, py) in enumerate(wide_peers):
             start(
-                tok_half.at[lax.rem(pxy, Y), pxy // Y], wide_in.at[xy], "wide", xy, sec,
-                pxy * Z + z, wide_slot + off,
+                tok_half.at[py, px], wide_in.at[xy], "wide", xy, sec, place(px, py, z),
+                wide_slot + off,
             )
 
     for px in ring(x, X):
@@ -241,8 +248,14 @@
         section = sec if index % 2 == 0 else far_sec
         copies.append(start(block, block, "y0", pz, section, place(x, other_y, z)))
 
-    for pz in near_first(z, Z):
-        copies.append(start(line(z), line(z), "z0", z, sec, place(x, y, pz)))
+    def along(steps):
+        return lax.rem(z + Z + steps, Z)
+
+    def send_line(block, pz, steps):
+        copies.append(start(block, block, "z0", pz, sec, place(x, y, along(steps))))
+
+    for steps in (1, -1, 2, -2):
+        send_line(line(z), z, steps)
     pass_y(0, z)
 
     load_down.wait()
@@ -270,6 +283,12 @@
         latent = lax.fori_loop(0, X, project, jnp.zeros((R, K), f32))
         active_ref[...] = (latent * sigmoid(latent)).astype(bf16)
         slope_ref[...] = silu_slope(latent)
+        for py in range(Y):
+            for index in range(X):
+                rows_at = pl.ds(index * y_part, y_part)
+                value = right_dot(active_ref[...], up_half[py, rows_at, :])
+                value = value + tok_half[py, index].astype(f32)
+                out_half[py, index] = value.astype(bf16)
 
     @pl.when(sec == 3)
     def _():
@@ -308,19 +327,33 @@
     def scale():
         lax.fori_loop(0, X, scale_rows, 0)
 
-    pl.when(sec != 0)(scale)
-
-    order = near_first(z, Z)
-    for index, pz in enumerate(order):
-        if index == 2:
-            arrive(planes.at[color1, x, other_y, 0:half_z], "y1", 0)
-            arrive(planes.at[color1, x, other_y, half_z:Z], "y1", 1)
-            slab = planes.at[color1, x, other_y]
-            for px in ring(x, X):
-                copies.append(start(slab, slab, "x1b", x, sec, place(px, y, z)))
-            copies.append(start(slab, slab, "d1b", x, sibling, dp))
+    order = [along(steps) for steps in (1, -1, 2, -2, 3, -3, 4)]
+    half_x = X // 2
+    for index, pz in enumerate(order[0:2]):
         arrive(line(pz), "z0", pz)
         pass_y(index + 1, pz)
+    for index, way in enumerate((1, -1)):
+        pz = along(2 * way)
+        arrive(line(pz), "z0", pz)
+        send_line(line(pz), pz, -way)
+        part = planes.at[color0, 0:half_x, y, pz] if way > 0 else planes.at[color0, half_x:X, y, pz]
+        copies.append(
+            start(part, part, "z4", index, sec, place(x, y, along(-2 * way)))
+        )
+        pass_y(index + 3, pz)
+    arrive(planes.at[color1, x, other_y, 0:half_z], "y1", 0)
+    arrive(planes.at[color1, x, other_y, half_z:Z], "y1", 1)
+    slab = planes.at[color1, x, other_y]
+    for px in ring(x, X):
+        copies.append(start(slab, slab, "x1b", x, sec, place(px, y, z)))
+    copies.append(start(slab, slab, "d1b", x, sibling, dp))
+    pl.when(sec != 0)(scale)
+    for index, pz in enumerate(order[4:6]):
+        arrive(line(pz), "z0", pz)
+        pass_y(index + 5, pz)
+    arrive(planes.at[color0, 0:half_x, y, order[6]], "z4", 0)
+    arrive(planes.at[color0, half_x:X, y, order[6]], "z4", 1)
+    pass_y(7, order[6])
     half = planes.at[color0, :, y]
     copies.append(start(half, half, "d0", 0, sibling, dp))
     for px in ring(x, X):
@@ -328,25 +361,40 @@
         arrive(slab, "x1a", px)
         copies.append(start(slab, slab, "d1a", px, sibling, dp))
 
+    late = []
+
+    def hop(group, src, dst, name, section):
+        late.append((group, src, sent[0]))
+        start(src, dst, name, 0, section, dp)
+
     their0, their1 = 2 - 2 * core, 3 - 2 * core
-    def products(py, add):
+    def products(py, add, last):
         for index in range(X):
             for color in range(4):
                 piece = planes[color, index, py].astype(f32).reshape(y_part, lanes).astype(bf16)
                 rows_at = slice(index * y_part, (index + 1) * y_part)
                 flat[rows_at, color * lanes : (color + 1) * lanes] = piece
 
+        def wide_code(rows):
+            value = jnp.zeros((R, C), f32)
+            for index in range(X):
+                rows_at = slice(index * y_part, (index + 1) * y_part)
+                value = value + plain_dot(rows[py, index], flat[rows_at, :])
+            add(tok_code, slice(0, C), value)
+
+        pl.when(sec == 0)(lambda: wide_code(out_half))
+        if last:
+            @pl.when(sec == 0)
+            def _():
+                code_out[...] = tok_code[...].astype(bf16)
+                hop("first", code_out, code_in, "code", 1)
+                hop("first", active_ref, active_in, "active", 1)
+
         @pl.when(sec != 3)
         def _():
             add(acc, slice(K + C, K + C + K), left_dot(flat[...], up_half[py]))
 
-        @pl.when(ends)
-        def _():
-            value = jnp.zeros((R, C), f32)
-            for index in range(X):
-                rows_at = slice(index * y_part, (index + 1) * y_part)
-                value = value + plain_dot(tok_half[py, index], flat[rows_at, :])
-            add(tok_code, slice(0, C), value)
+        pl.when(sec == 3)(lambda: wide_code(tok_half))
 
         @pl.when(sec != 0)
         def _():
@@ -363,23 +411,24 @@
     arrive(planes.at[their1, x, y], "d1a", x)
     for px in ring(x, X):
         arrive(planes.at[their1, px, y], "d1a", px)
-    products(y, put)
-
-    for index, pz in enumerate([z] + order):
-        arrive(planes.at[color0, :, other_y, pz], "y0", pz)
-    half = planes.at[color0, :, other_y]
-    copies.append(start(half, half, "d0", 1, sibling, dp))
+    products(y, put, False)
+
+    for pz in [z] + order:
+        block = planes.at[color0, :, other_y, pz]
+        arrive(block, "y0", pz)
+        copies.append(start(block, block, "d0z", pz, sibling, dp))
     for px in ring(x, X):
         slab = planes.at[color1, px, other_y]
         arrive(slab, "x1b", px)
         copies.append(start(slab, slab, "d1b", px, sibling, dp))
 
-    arrive(planes.at[their0, :, other_y], "d0", 1)
+    for pz in [z] + order:
+        arrive(planes.at[their0, :, other_y, pz], "d0z", pz)
     arrive(planes.at[their1, x, other_y], "d1b", x)
     for px in ring(x, X):
         arrive(planes.at[their1, px, other_y], "d1b", px)
 
-    products(other_y, add_to)
+    products(other_y, add_to, True)
 
     @pl.when(sec != 3)
     def _():
@@ -389,81 +438,104 @@
     def _():
         weights[:, 0 : K + C] = acc[:, 0 : K + C].astype(bf16)
 
-    def forward():
-        code = code_in[...]
-        both = plain_dot(code, weights[:, 0 : K + C])
-        grid = both[:, K:]
+    XY = X * Y
+    def forward(code, weight):
+        grid = plain_dot(code, weights[:, K : K + C])
         square = jnp.sum(code.astype(f32) * grid, axis=-1, keepdims=True) * (ratio * ratio / D)
         inverse = lax.rsqrt(square + epsilon)
-        latent = ratio * inverse * both[:, 0:K]
+        latent = ratio * inverse * plain_dot(code, weight)
         active = (latent * sigmoid(latent)).astype(bf16)
-        return code, grid, inverse, latent, active
-
-    def backward(inner, grid, inverse, latent, d_latent):
-        weight = jnp.sum(d_latent.astype(f32) * latent, axis=-1, keepdims=True)
-        weight = weight * inverse * inverse * (ratio / D)
-        through = right_dot(d_latent, weights[:, 0:K])
-        return (ratio * (inner + inverse * through - weight * grid)).astype(bf16)
-
-    late = []
-
-    def hop(group, src, dst, name, section):
-        late.append((group, src, sent[0]))
-        start(src, dst, name, 0, section, dp)
+        return grid, inverse, latent, active
+
+    def backward(inner, grid, inverse, latent, d_latent, weight):
+        share = jnp.sum(d_latent.astype(f32) * latent, axis=-1, keepdims=True)
+        share = share * inverse * inverse * (ratio / D)
+        through = right_dot(d_latent, weight)
+        return (ratio * (inner + inverse * through - share * grid)).astype(bf16)
+
+    def next_code(grid, active):
+        return (ratio * grid + right_dot(active, weights[:, K + C :])).astype(bf16)
+
+    def scale_latent(d_latent, inverse):
+        return (d_latent.astype(f32) * (ratio * inverse)).astype(bf16)
+
+    def send_factor(name):
+        for pxy in [xy] + xy_ring:
+            late.append((name, factor, sent[0]))
+            start(factor, factor_in.at[xy], "factor", xy, sibling, pxy * Z + z)
 
     @pl.when(sec == 0)
     def _():
-        result = tok_code[...] + right_dot(active_ref[...], weights[:, K + C :])
-        code_out[...] = result.astype(bf16)
-        hop("first", code_out, code_in, "code", 1)
-        hop("first", active_ref, active_in, "active", 1)
-
-    @pl.when(middle)
-    def _():
+        latent_ref[...] = slope_ref[...] * inv_ref[...]
+        hop("first", weights.at[:, K + C :], lead_weight, "lead_weight", 1)
+        hop("first", latent_ref, lead_slope, "lead_slope", 1)
+        scale()
+
+    @pl.when(sec == 3)
+    def _():
+        hop("last", weights.at[:, 0:K], lead_weight, "lead_weight", 2)
+        hop("last", latent_ref, lead_slope, "lead_slope", 2)
+        hop("last", tok_code, lead_code, "lead_code", 2)
         arrive(code_in, "code", 0)
-        code, grid, inverse, latent, active = forward()
-        result = ratio * grid + right_dot(active, weights[:, K + C :])
-        code_out[...] = result.astype(bf16)
-        hop("middle", code_out, code_in, "code", sec + 1)
+        arrive(scaled, "scaled", 0)
+        down_part[...] = left_dot(code_in[...], scaled[...]).astype(bf16).reshape(down_part.shape)
+        arrive(active_in, "active", 0)
+        arrive(back_in, "back", 0)
+        up_part[...] = left_dot(back_in[...], active_in[...]).astype(bf16).reshape(up_part.shape)
+
+    @pl.when(sec == 1)
+    def _():
+        arrive(code_in, "code", 0)
+        grid, inverse, latent, active = forward(code_in[...], weights[:, 0:K])
+        code_out[...] = next_code(grid, active)
+        hop("second", code_out, code_in, "code", 2)
         active_ref[...] = active
-        hop("middle", active_ref, active_in, "active", sec + 1)
-        code_grid[...] = grid
-        inv_ref[...] = inverse
-        latent_ref[...] = latent
-        slope_ref[...] = silu_slope(latent)
-
-    def code_sums(code, inverse, d_latent):
-        scaled = (d_latent.astype(f32) * (ratio * inverse)).astype(bf16)
-        down_part[...] = left_dot(code, scaled).astype(bf16).reshape(down_part.shape)
-
-    @pl.when(sec == 3)
-    def _():
-        arrive(code_in, "code", 0)
-        code, grid, inverse, latent, active = forward()
-        factor[...] = active
-        d_latent = (latent_ref[...] * silu_slope(latent)).astype(bf16)
-        back_out[...] = backward(tok_code[...], grid, inverse, latent, d_latent)
-        hop("last", back_out, back_in, "back", 2)
-        code_sums(code, inverse, d_latent)
-
-    @pl.when(middle)
-    def _():
+        hop("second", active_ref, active_in, "active", 2)
+        slope = silu_slope(latent)
+        arrive(lead_weight, "lead_weight", 0)
+        arrive(lead_slope, "lead_slope", 0)
+        arrive(active_in, "active", 0)
         arrive(back_in, "back", 0)
         both = plain_dot(back_in[...], weights[:, K:])
-        inverse = inv_ref[...]
-        d_latent = (both[:, C:] * slope_ref[...]).astype(bf16)
-        back_out[...] = backward(both[:, 0:C], code_grid[...], inverse, latent_ref[...], d_latent)
-        hop("middle", back_out, back_in, "back", sec - 1)
-        code_sums(code_in[...], inverse, d_latent)
-
-    @pl.when(sec == 0)
-    def _():
-        scale()
-        arrive(back_in, "back", 0)
-        d_latent = (plain_dot(back_in[...], weights[:, K + C :]) * slope_ref[...]).astype(bf16)
-        factor[...] = (d_latent.astype(f32) * inv_ref[...]).astype(bf16)
-
-    XY = X * Y
+        d_latent = (both[:, C:] * slope).astype(bf16)
+        back = backward(both[:, 0:C], grid, inverse, latent, d_latent, weights[:, 0:K])
+        factor[...] = (plain_dot(back, lead_weight[...]) * lead_slope[...]).astype(bf16)
+        down = left_dot(code_in[...], scale_latent(d_latent, inverse))
+        down_part[...] = down.astype(bf16).reshape(down_part.shape)
+        up_part[...] = left_dot(back, active_in[...]).astype(bf16).reshape(up_part.shape)
+
+    @pl.when(sec == 2)
+    def _():
+        arrive(code_in, "code", 0)
+        grid, inverse, latent, active = forward(code_in[...], weights[:, 0:K])
+        code = next_code(grid, active)
+        code_out[...] = code
+        hop("third", code_out, code_in, "code", 3)
+        active_ref[...] = active
+        hop("third", active_ref, active_in, "active", 3)
+        arrive(lead_weight, "lead_weight", 0)
+        arrive(lead_slope, "lead_slope", 0)
+        arrive(lead_code, "lead_code", 0)
+        last_grid, last_inverse, last_latent, last_active = forward(code, lead_weight[...])
+        last = (lead_slope[...] * silu_slope(last_latent)).astype(bf16)
+        turn = backward(
+            lead_code[...], last_grid, last_inverse, last_latent, last, lead_weight[...]
+        )
+        both = plain_dot(turn, weights[:, K:])
+        d_latent = (both[:, C:] * silu_slope(latent)).astype(bf16)
+        back = backward(both[:, 0:C], grid, inverse, latent, d_latent, weights[:, 0:K])
+        back_out[...] = back
+        hop("third", back_out, back_in, "back", 1)
+        turn_out[...] = turn
+        hop("third", turn_out, back_in, "back", 3)
+        scaled_out[...] = scale_latent(last, last_inverse)
+        hop("third", scaled_out, scaled, "scaled", 3)
+        factor[...] = last_active
+        down = left_dot(code_in[...], scale_latent(d_latent, inverse))
+        down_part[...] = down.astype(bf16).reshape(down_part.shape)
+        arrive(active_in, "active", 0)
+        up_part[...] = left_dot(back, active_in[...]).astype(bf16).reshape(up_part.shape)
+
     xy_peers = [(pxy, pxy * Z + z) for pxy in xy_ring]
     z_peers = [(pz, place(x, y, pz)) for pz in near_first(z, Z)]
     pending_rest, pending_ends = [], []
@@ -487,22 +559,21 @@
     @pl.when(rest)
     def _():
         spread(lambda peer: down_part.at[peer], down_in, "down_a", z, z_peers, pending_rest)
-        arrive(active_in, "active", 0)
-        up_part[...] = left_dot(back_out[...], active_in[...]).astype(bf16).reshape(up_part.shape)
         spread(lambda peer: up_part.at[peer], up_parts, "up_a", xy, xy_peers, pending_rest)
-
-    @pl.when(ends)
-    def _():
-        spread(lambda peer: factor, factor_in, "factor", xy, xy_peers, pending_ends)
 
     @pl.when(rest)
     def _():
         up_line[...] = gathered(up_part[xy], up_parts, "up_a", xy_peers).astype(bf16)
         spread(lambda peer: up_line, up_lines, "up_b", z, z_peers, pending_rest)
 
+    @pl.when(jnp.logical_not(ends))
+    def _():
+        send_factor("lead")
+
     @pl.when(ends)
     def _():
-        value = left_dot(tok_half[y, x], factor[...])
+        arrive(factor_in.at[xy], "factor", xy)
+        value = left_dot(tok_half[y, x], factor_in[xy])
         for pxy, _ in xy_peers:
             arrive(wide_in.at[pxy], "wide", pxy)
             arrive(factor_in.at[pxy], "factor", pxy)
@@ -572,7 +643,9 @@
         for off in range(XY - 1):
             left(wide_in.at[0], wide_slot + off)
 
-    for group, chosen in (("first", sec == 0), ("middle", middle), ("last", sec == 3), ("rest", rest)):
+    groups = [("first", sec == 0), ("second", sec == 1), ("third", sec == 2), ("last", sec == 3)]
+    groups += [("rest", rest), ("lead", jnp.logical_not(ends))]
+    for group, chosen in groups:
         @pl.when(chosen)
         def _():
             for which, src, slot in late:
@@ -604,7 +677,7 @@
     block_rows = C // (X * Y)
     any_space = pl.BlockSpec(memory_space=pl.ANY)
     vmem = pl.BlockSpec(memory_space=pltpu.VMEM)
-    recv_count = 5 * X + 7 * Z + 8 + 5 * X * Y
+    recv_count = 5 * X + 8 * Z + 14 + 5 * X * Y
     scratch = [
         ((micro, rows, D), bf16),
         ((1, D), f32),
@@ -617,6 +690,7 @@
         ((4, X, Y, Z, own, lanes), bf16),
         ((D // Y, C), bf16),
         ((Y, X, R, chunk // Y), bf16),
+        ((Y, X, R, chunk // Y), bf16),
         ((C, 2 * K + C), f32),
         ((C, 2 * K + C), bf16),
         ((R, C), f32),
@@ -624,11 +698,16 @@
         ((R, K), bf16),
         ((R, 1), f32),
         ((R, K), f32),
-        ((R, C), f32),
         ((R, C), bf16),
         ((R, C), bf16),
         ((R, C), bf16),
         ((R, C), bf16),
+        ((R, C), bf16),
+        ((R, K), bf16),
+        ((R, K), bf16),
+        ((C, K), bf16),
+        ((R, K), f32),
+        ((R, C), f32),
         ((R, K), bf16),
         ((X * Y, R, chunk // Y), bf16),
         ((R, K), bf16),

time: 79.4 us -> 76.1 us (0.958)
  Pallas kernels: 78.7 us -> 75.4 us
    pallas_call x1, Pallas kernels: 74 us -> 70.8 us  [on_device(): pl.pallas_call(functools.partial(kernel, (X, Y, Z)), out_shape=(jax.Shape...]
where the time goes in v4:
time: 76.1 us
  Pallas kernels  75.4 us (99%)
    pallas_call x1, Pallas kernels, on_device(): pl.pallas_call(functools.partial(kernel, (X, Y, Z)), out_shape=(jax.Shape...  70.8 us
    pallas_call x1, Pallas kernels, on_device(): pl.pallas_call(hand_out, out_shape=(jax.ShapeDtypeStruct((own, K), f32),...  4.62 us

profile of v4, /device:TPU:1, one launch (start us, length us, event | category | flops | bytes accessed | tf_op | source)
XLA Modules:
  0.0 76.1 jit_solution(9443903799680034297)
XLA Ops:
  0.6 70.8 %shard_map.85 = (f32[56,256]{1,0:T(8,128)}, f32[56,256]{1,0:T(8,128)}, f32[1,56]{1,0:T(1,128)}) custom-call(bf16[2,64,3584]{2,1,0:T(8,128)(2,1)} %hidden.1, bf16[2,64,3584]{2,1,0:T(8,128)(2,1)} %head.1, bf16[3584,256]{1,0:T(8,128)(2,1)} %bitcast.6, bf16[3584,256]{1,0:T(8,128)(2,1)} %bitcast.7, f32[1,3584]{1,0:T(1,128)} %bitcast.8, bf16[56,512]{1,0:T(8,128)(2,1)} %codec_hbm.1), custom_call_target="tpu_custom_call" | custom-call | tf_op jit(solution)/shard_map/pallas_call | solution.py:731
  71.4 4.6 %shard_map.86 = (f32[56,256]{1,0:T(8,128)}, f32[56,256]{1,0:T(8,128)}, f32[1,56]{1,0:T(1,128)}) custom-call(f32[56,256]{1,0:T(8,128)} %get-tuple-element.9.down, f32[56,256]{1,0:T(8,128)} %get-tuple-element.10.up, f32[1,56]{1,0:T(1,128)} %get-tuple-element.11.gain), custom_call_target="tpu_custom_call" | custom-call | tf_op jit(solution)/shard_map/pallas_call | solution.py:750

commit v5 on v4

--- a/solution.py
+++ b/solution.py
@@ -209,7 +209,7 @@
     half_z = Z // 2
     copies = []
     mine = planes.at[color0, x, y, z]
-    for px in ring(x, X):
+    for px in near_first(x, X)[::-1]:
         copies.append(start(mine, mine, "x0", x, sec, place(px, y, z)))
     mine = planes.at[color1, x, y, z]
     for pz in near_first(z, Z):
@@ -305,7 +305,7 @@
     copies.append(start(near, near, "y1", 0, sec, place(x, other_y, z)))
     copies.append(start(far, far, "y1", 1, far_sec, place(x, other_y, z)))
     slab = planes.at[color1, x, y]
-    for px in ring(x, X):
+    for px in near_first(x, X)[::-1]:
         copies.append(start(slab, slab, "x1a", x, sec, place(px, y, z)))
     copies.append(start(slab, slab, "d1a", x, sibling, dp))
 
@@ -344,7 +344,7 @@
     arrive(planes.at[color1, x, other_y, 0:half_z], "y1", 0)
     arrive(planes.at[color1, x, other_y, half_z:Z], "y1", 1)
     slab = planes.at[color1, x, other_y]
-    for px in ring(x, X):
+    for px in near_first(x, X)[::-1]:
         copies.append(start(slab, slab, "x1b", x, sec, place(px, y, z)))
     copies.append(start(slab, slab, "d1b", x, sibling, dp))
     pl.when(sec != 0)(scale)
@@ -464,6 +464,30 @@
             late.append((name, factor, sent[0]))
             start(factor, factor_in.at[xy], "factor", xy, sibling, pxy * Z + z)
 
+    far_x = sorted(range(X), key=lambda off: -min(off, X - off))
+    xy_far = [(lax.rem(x + off, X), other_y) for off in far_x]
+    xy_far += [(lax.rem(x + off, X), y) for off in far_x[:-1]]
+    xy_peers = [(px * Y + py, place(px, py, z)) for px, py in xy_far]
+    z_peers = [(pz, place(x, y, pz)) for pz in near_first(z, Z)[::-1]]
+    pending_rest, pending_ends, pending_back, first_slot = [], [], [], {}
+
+    def spread(ref_of, landings, name, mine, peers, pending):
+        if name not in first_slot:
+            first_slot[name] = sent[0]
+            sent[0] += len(peers)
+            pending.extend((landings, first_slot[name] + n) for n in range(len(peers)))
+        for n, (peer, peer_dp) in enumerate(peers):
+            start(
+                ref_of(peer), landings.at[mine], name, mine, sec, peer_dp, first_slot[name] + n
+            )
+
+    def gathered(first, landing, name, peers):
+        value = first.astype(f32)
+        for peer, _ in peers:
+            arrive(landing.at[peer], name, peer)
+            value = value + landing[peer].astype(f32)
+        return value
+
     @pl.when(sec == 0)
     def _():
         latent_ref[...] = slope_ref[...] * inv_ref[...]
@@ -479,9 +503,11 @@
         arrive(code_in, "code", 0)
         arrive(scaled, "scaled", 0)
         down_part[...] = left_dot(code_in[...], scaled[...]).astype(bf16).reshape(down_part.shape)
+        spread(lambda peer: down_part.at[peer], down_in, "down_a", z, z_peers, pending_rest)
         arrive(active_in, "active", 0)
         arrive(back_in, "back", 0)
         up_part[...] = left_dot(back_in[...], active_in[...]).astype(bf16).reshape(up_part.shape)
+        spread(lambda peer: up_part.at[peer], up_parts, "up_a", xy, xy_peers, pending_rest)
 
     @pl.when(sec == 1)
     def _():
@@ -499,10 +525,12 @@
         both = plain_dot(back_in[...], weights[:, K:])
         d_latent = (both[:, C:] * slope).astype(bf16)
         back = backward(both[:, 0:C], grid, inverse, latent, d_latent, weights[:, 0:K])
-        factor[...] = (plain_dot(back, lead_weight[...]) * lead_slope[...]).astype(bf16)
+        up_part[...] = left_dot(back, active_in[...]).astype(bf16).reshape(up_part.shape)
+        spread(lambda peer: up_part.at[peer], up_parts, "up_a", xy, xy_peers, pending_rest)
         down = left_dot(code_in[...], scale_latent(d_latent, inverse))
         down_part[...] = down.astype(bf16).reshape(down_part.shape)
-        up_part[...] = left_dot(back, active_in[...]).astype(bf16).reshape(up_part.shape)
+        spread(lambda peer: down_part.at[peer], down_in, "down_a", z, z_peers, pending_rest)
+        factor[...] = (plain_dot(back, lead_weight[...]) * lead_slope[...]).astype(bf16)
 
     @pl.when(sec == 2)
     def _():
@@ -518,6 +546,8 @@
         arrive(lead_code, "lead_code", 0)
         last_grid, last_inverse, last_latent, last_active = forward(code, lead_weight[...])
         last = (lead_slope[...] * silu_slope(last_latent)).astype(bf16)
+        scaled_out[...] = scale_latent(last, last_inverse)
+        hop("third", scaled_out, scaled, "scaled", 3)
         turn = backward(
             lead_code[...], last_grid, last_inverse, last_latent, last, lead_weight[...]
         )
@@ -528,38 +558,17 @@
         hop("third", back_out, back_in, "back", 1)
         turn_out[...] = turn
         hop("third", turn_out, back_in, "back", 3)
-        scaled_out[...] = scale_latent(last, last_inverse)
-        hop("third", scaled_out, scaled, "scaled", 3)
         factor[...] = last_active
+        arrive(active_in, "active", 0)
+        up_part[...] = left_dot(back, active_in[...]).astype(bf16).reshape(up_part.shape)
+        spread(lambda peer: up_part.at[peer], up_parts, "up_a", xy, xy_peers, pending_rest)
         down = left_dot(code_in[...], scale_latent(d_latent, inverse))
         down_part[...] = down.astype(bf16).reshape(down_part.shape)
-        arrive(active_in, "active", 0)
-        up_part[...] = left_dot(back, active_in[...]).astype(bf16).reshape(up_part.shape)
-
-    xy_peers = [(pxy, pxy * Z + z) for pxy in xy_ring]
-    z_peers = [(pz, place(x, y, pz)) for pz in near_first(z, Z)]
-    pending_rest, pending_ends = [], []
-
-    def spread(ref_of, landings, name, mine, peers, pending):
-        for peer, peer_dp in peers:
-            slot = sent[0]
-            start(ref_of(peer), landings.at[mine], name, mine, sec, peer_dp)
-            pending.append((landings, slot))
-
-    def gathered(first, landing, name, peers):
-        value = first.astype(f32)
-        for peer, _ in peers:
-            arrive(landing.at[peer], name, peer)
-            value = value + landing[peer].astype(f32)
-        return value
+        spread(lambda peer: down_part.at[peer], down_in, "down_a", z, z_peers, pending_rest)
 
     rest = sec != 0
+    back_half = sec >= 2
     load_codec.wait()
-
-    @pl.when(rest)
-    def _():
-        spread(lambda peer: down_part.at[peer], down_in, "down_a", z, z_peers, pending_rest)
-        spread(lambda peer: up_part.at[peer], up_parts, "up_a", xy, xy_peers, pending_rest)
 
     @pl.when(rest)
     def _():
@@ -586,13 +595,26 @@
         down_block[...] = gathered(down_part[z], down_in, "down_a", z_peers).astype(bf16)
         spread(lambda peer: down_block, down_blocks, "down_b", xy, xy_peers, pending_rest)
         up_sum[xy] = gathered(up_line[...], up_lines, "up_b", z_peers).astype(bf16)
-        spread(lambda peer: up_sum.at[xy], up_sum, "up_c", xy, xy_peers, pending_rest)
+
+        @pl.when(sec == 1)
+        def _():
+            for pxy in [xy] + xy_ring:
+                late.append(("second", up_line, sent[0]))
+                start(up_sum.at[xy], up_sum.at[xy], "up_c", xy, sibling, pxy * Z + z)
+
+        @pl.when(back_half)
+        def _():
+            spread(lambda peer: up_sum.at[xy], up_sum, "up_c", xy, xy_peers, pending_back)
+
         down_sum[z] = gathered(down_block[...], down_blocks, "down_b", xy_peers).astype(bf16)
         spread(lambda peer: down_sum.at[z], down_sum, "down_c", z, z_peers, pending_rest)
+
+    @pl.when(back_half)
+    def _():
         for pxy, _ in xy_peers:
             arrive(up_sum.at[pxy], "up_c", pxy)
         up_result[...] = plain_dot(codec[...], up_sum[...].reshape(C, K))
-        hop("rest", up_result, up_results, "up", sec - 1)
+        hop("back_half", up_result, up_results, "up", sec - 1)
 
     own_rows = pl.ds(pl.multiple_of(dp * own, 8), own)
 
@@ -626,7 +648,13 @@
     def _():
         out_up[...] = wide_sum[...]
 
-    @pl.when(sec != 3)
+    @pl.when(sec == 0)
+    def _():
+        for pxy in [xy] + xy_ring:
+            arrive(up_sum.at[pxy], "up_c", pxy)
+        out_up[...] = plain_dot(codec[...], up_sum[...].reshape(C, K))
+
+    @pl.when(jnp.logical_not(ends))
     def _():
         arrive(up_results, "up", 0)
         out_up[...] = up_results[...]
@@ -643,7 +671,12 @@
         for off in range(XY - 1):
             left(wide_in.at[0], wide_slot + off)
 
-    groups = [("first", sec == 0), ("second", sec == 1), ("third", sec == 2), ("last", sec == 3)]
+    @pl.when(back_half)
+    def _():
+        for landing, slot in pending_back:
+            left(landing.at[0], slot)
+
+    groups = [("back_half", back_half), ("first", sec == 0), ("second", sec == 1), ("third", sec == 2), ("last", sec == 3)]
     groups += [("rest", rest), ("lead", jnp.logical_not(ends))]
     for group, chosen in groups:
         @pl.when(chosen)

time: 76.1 us -> 74.6 us (0.980)
  Pallas kernels: 75.4 us -> 73.9 us
    pallas_call x1, Pallas kernels: 70.8 us -> 69.3 us  [on_device(): pl.pallas_call(functools.partial(kernel, (X, Y, Z)), out_shape=(jax.Shape...]
where the time goes in v5:
time: 74.6 us; the launch traced here: 74.5 us
  Pallas kernels  73.9 us (99%)
    pallas_call x1, Pallas kernels, on_device(): pl.pallas_call(functools.partial(kernel, (X, Y, Z)), out_shape=(jax.Shape...  69.3 us
    pallas_call x1, Pallas kernels, on_device(): pl.pallas_call(hand_out, out_shape=(jax.ShapeDtypeStruct((own, K), f32),...  4.62 us

profile of v5, /device:TPU:1, one launch (start us, length us, event | category | flops | bytes accessed | tf_op | source)
XLA Modules:
  0.0 74.5 jit_solution(8032229524499483788)
XLA Ops:
  0.6 69.3 %shard_map.85 = (f32[56,256]{1,0:T(8,128)}, f32[56,256]{1,0:T(8,128)}, f32[1,56]{1,0:T(1,128)}) custom-call(bf16[2,64,3584]{2,1,0:T(8,128)(2,1)} %hidden.1, bf16[2,64,3584]{2,1,0:T(8,128)(2,1)} %head.1, bf16[3584,256]{1,0:T(8,128)(2,1)} %bitcast.6, bf16[3584,256]{1,0:T(8,128)(2,1)} %bitcast.7, f32[1,3584]{1,0:T(1,128)} %bitcast.8, bf16[56,512]{1,0:T(8,128)(2,1)} %codec_hbm.1), custom_call_target="tpu_custom_call" | custom-call | tf_op jit(solution)/shard_map/pallas_call | solution.py:764
  69.9 4.6 %shard_map.86 = (f32[56,256]{1,0:T(8,128)}, f32[56,256]{1,0:T(8,128)}, f32[1,56]{1,0:T(1,128)}) custom-call(f32[56,256]{1,0:T(8,128)} %get-tuple-element.9.down, f32[56,256]{1,0:T(8,128)} %get-tuple-element.10.up, f32[1,56]{1,0:T(1,128)} %get-tuple-element.11.gain), custom_call_target="tpu_custom_call" | custom-call | tf_op jit(solution)/shard_map/pallas_call | solution.py:783

commit v6 on v5

--- a/solution.py
+++ b/solution.py
@@ -442,7 +442,7 @@
     def forward(code, weight):
         grid = plain_dot(code, weights[:, K : K + C])
         square = jnp.sum(code.astype(f32) * grid, axis=-1, keepdims=True) * (ratio * ratio / D)
-        inverse = lax.rsqrt(square + epsilon)
+        inverse = lax.rsqrt(jnp.maximum(square, 0.0) + epsilon)
         latent = ratio * inverse * plain_dot(code, weight)
         active = (latent * sigmoid(latent)).astype(bf16)
         return grid, inverse, latent, active

time: 74.6 us -> 74.6 us (level)
  no operation moved by 1% of the time
where the time goes in v6:
time: 74.6 us; the launch traced here: 74.5 us
  Pallas kernels  73.9 us (99%)
    pallas_call x1, Pallas kernels, on_device(): pl.pallas_call(functools.partial(kernel, (X, Y, Z)), out_shape=(jax.Shape...  69.3 us
    pallas_call x1, Pallas kernels, on_device(): pl.pallas_call(hand_out, out_shape=(jax.ShapeDtypeStruct((own, K), f32),...  4.62 us

profile of v6, /device:TPU:1, one launch (start us, length us, event | category | flops | bytes accessed | tf_op | source)
XLA Modules:
  0.0 74.5 jit_solution(17153852378255778118)
XLA Ops:
  0.6 69.3 %shard_map.85 = (f32[56,256]{1,0:T(8,128)}, f32[56,256]{1,0:T(8,128)}, f32[1,56]{1,0:T(1,128)}) custom-call(bf16[2,64,3584]{2,1,0:T(8,128)(2,1)} %hidden.1, bf16[2,64,3584]{2,1,0:T(8,128)(2,1)} %head.1, bf16[3584,256]{1,0:T(8,128)(2,1)} %bitcast.6, bf16[3584,256]{1,0:T(8,128)(2,1)} %bitcast.7, f32[1,3584]{1,0:T(1,128)} %bitcast.8, bf16[56,512]{1,0:T(8,128)(2,1)} %codec_hbm.1), custom_call_target="tpu_custom_call" | custom-call | tf_op jit(solution)/shard_map/pallas_call | solution.py:764
  69.9 4.6 %shard_map.86 = (f32[56,256]{1,0:T(8,128)}, f32[56,256]{1,0:T(8,128)}, f32[1,56]{1,0:T(1,128)}) custom-call(f32[56,256]{1,0:T(8,128)} %get-tuple-element.9.down, f32[56,256]{1,0:T(8,128)} %get-tuple-element.10.up, f32[1,56]{1,0:T(1,128)} %get-tuple-element.11.gain), custom_call_target="tpu_custom_call" | custom-call | tf_op jit(solution)/shard_map/pallas_call | solution.py:783

commit v7 on v6

--- a/solution.py
+++ b/solution.py
@@ -130,7 +130,7 @@
 
     names = [
         ("x0", X), ("z0", Z), ("y0", Z), ("z1", Z), ("y1", 2), ("x1a", X), ("x1b", X),
-        ("z4", 2), ("d0", 1), ("d0z", Z), ("d1a", X), ("d1b", X), ("code", 1), ("back", 1), ("active", 1), ("up", 1),
+        ("z4", 2), ("d0", Z), ("d0z", Z), ("d1a", X), ("d1b", X), ("code", 1), ("back", 1), ("active", 1), ("up", 1),
         ("scaled", 1), ("lead_weight", 1), ("lead_slope", 1), ("lead_code", 1),
         ("wide", X * Y), ("factor", X * Y), ("big", Z), ("down_a", Z), ("down_b", X * Y),
         ("down_c", Z), ("up_a", X * Y), ("up_b", Z), ("up_c", X * Y),
@@ -247,6 +247,7 @@
         block = line(pz)
         section = sec if index % 2 == 0 else far_sec
         copies.append(start(block, block, "y0", pz, section, place(x, other_y, z)))
+        copies.append(start(block, block, "d0", pz, sibling, dp))
 
     def along(steps):
         return lax.rem(z + Z + steps, Z)
@@ -354,8 +355,6 @@
     arrive(planes.at[color0, 0:half_x, y, order[6]], "z4", 0)
     arrive(planes.at[color0, half_x:X, y, order[6]], "z4", 1)
     pass_y(7, order[6])
-    half = planes.at[color0, :, y]
-    copies.append(start(half, half, "d0", 0, sibling, dp))
     for px in ring(x, X):
         slab = planes.at[color1, px, y]
         arrive(slab, "x1a", px)
@@ -407,7 +406,8 @@
     def add_to(ref, columns, value):
         ref[:, columns] += value
 
-    arrive(planes.at[their0, :, y], "d0", 0)
+    for pz in [z] + order:
+        arrive(planes.at[their0, :, y, pz], "d0", pz)
     arrive(planes.at[their1, x, y], "d1a", x)
     for px in ring(x, X):
         arrive(planes.at[their1, px, y], "d1a", px)
@@ -710,7 +710,7 @@
     block_rows = C // (X * Y)
     any_space = pl.BlockSpec(memory_space=pl.ANY)
     vmem = pl.BlockSpec(memory_space=pltpu.VMEM)
-    recv_count = 5 * X + 8 * Z + 14 + 5 * X * Y
+    recv_count = 5 * X + 9 * Z + 13 + 5 * X * Y
     scratch = [
         ((micro, rows, D), bf16),
         ((1, D), f32),

time: 74.6 us -> 74.7 us (level)
  no operation moved by 1% of the time
where the time goes in v7:
time: 74.7 us; the launch traced here: 74.6 us
  Pallas kernels  74 us (99%)
    pallas_call x1, Pallas kernels, on_device(): pl.pallas_call(functools.partial(kernel, (X, Y, Z)), out_shape=(jax.Shape...  69.3 us
    pallas_call x1, Pallas kernels, on_device(): pl.pallas_call(hand_out, out_shape=(jax.ShapeDtypeStruct((own, K), f32),...  4.62 us

profile of v7, /device:TPU:1, one launch (start us, length us, event | category | flops | bytes accessed | tf_op | source)
XLA Modules:
  0.0 74.6 jit_solution(900528958116191658)
XLA Ops:
  0.6 69.3 %shard_map.85 = (f32[56,256]{1,0:T(8,128)}, f32[56,256]{1,0:T(8,128)}, f32[1,56]{1,0:T(1,128)}) custom-call(bf16[2,64,3584]{2,1,0:T(8,128)(2,1)} %hidden.1, bf16[2,64,3584]{2,1,0:T(8,128)(2,1)} %head.1, bf16[3584,256]{1,0:T(8,128)(2,1)} %bitcast.6, bf16[3584,256]{1,0:T(8,128)(2,1)} %bitcast.7, f32[1,3584]{1,0:T(1,128)} %bitcast.8, bf16[56,512]{1,0:T(8,128)(2,1)} %codec_hbm.1), custom_call_target="tpu_custom_call" | custom-call | tf_op jit(solution)/shard_map/pallas_call | solution.py:764
  70.0 4.6 %shard_map.86 = (f32[56,256]{1,0:T(8,128)}, f32[56,256]{1,0:T(8,128)}, f32[1,56]{1,0:T(1,128)}) custom-call(f32[56,256]{1,0:T(8,128)} %get-tuple-element.9.down, f32[56,256]{1,0:T(8,128)} %get-tuple-element.10.up, f32[1,56]{1,0:T(1,128)} %get-tuple-element.11.gain), custom_call_target="tpu_custom_call" | custom-call | tf_op jit(solution)/shard_map/pallas_call | solution.py:783
